TPU v7x, 512 devices: a whole 4x4x16 slice. The times are simulated.
512 devices in a mesh: sensor: 64 (over z, y), tm: 8 (over x, core).
Axes of the slice: x: 4, y: 4, z: 16, core: 2. Of those that a mesh axis runs over, the one named last changes fastest.
Arguments:
- signal: bfloat16 [64, 512, 8192], P(None, 'tm', 'sensor'), may hold values from -6 to 6
- conv_weight: bfloat16 [128, 128], replicated, may hold values from -0.5 to 0.5
- conv_bias: float32 [128], replicated, may hold values from -3 to 3
- diff_weight: bfloat16 [64, 192], replicated, may hold values from -1.5 to 1.5
- neighbour_index: int32 [8192, 32], P('sensor'), may hold values from 0 to 8191, as said below
- neighbour_count: int32 [8192], P('sensor'), may hold values from 2 to 32, as said below
- edge_weight: float32 [8192, 32], P('sensor'), may hold values from 0.05 to 10
- cotangent: bfloat16 [64, 512, 8192], P(None, 'tm', 'sensor'), may hold values from -6 to 6
Outputs:
- output: bfloat16 [64, 512, 8192], P(None, 'tm', 'sensor')
- grad_signal: bfloat16 [64, 512, 8192], P(None, 'tm', 'sensor')
Inputs may be any that keep to these rules, and one draw needn't show every extreme that they name: `neighbour_index`: sensor s belongs to partition s // 128. The live slots of a sensor name distinct sensors other than itself. The sensors of one partition name at most 4 distinct sensors of any other partition in live slots, and at most 4 sensors of one partition have a live slot naming a sensor of any one other partition; in every draw some partition names exactly 4 sensors of every other partition. The live slots of a sensor are its first neighbour_count slots; some sensor of every partition has all 32 live.
All inputs are finite; a program needn't handle non-finite values.
Results may differ from a plain program's by a relative error of at most 0.0045.
Values may be sent and summed in bfloat16 or wider, within the bound.
No kernel may reach another device: no remote copies, remote signals or barrier semaphores. Data moves between devices by JAX's collectives and lax.ppermute only.
A program may use at most 128 MiB of HBM per device.

v0:
```python
import jax
import jax.numpy as jnp
from jax import lax
from jax.sharding import PartitionSpec as P

DILATION = 8
CAPACITY = 4


def from_behind(value, axis, by):
    count = lax.axis_size(axis)
    pairs = [(i, i + by) for i in range(count) if 0 <= i + by < count]
    return lax.ppermute(value, axis, pairs)


def compact_list(flags, peer_count, sensor_count):
    placed = jnp.cumsum(flags, axis=1) - 1
    peer_ids = lax.broadcasted_iota(jnp.int32, (peer_count, sensor_count), 0)
    member_ids = lax.broadcasted_iota(jnp.int32, (peer_count, sensor_count), 1)
    listing = jnp.full((peer_count, CAPACITY), -1, jnp.int32)
    listing = listing.at[peer_ids, jnp.where(flags > 0, placed, CAPACITY)].set(
        member_ids, mode="drop"
    )
    return (placed, listing)


def per_device(
    signal,
    conv_weight,
    conv_bias,
    diff_weight,
    neighbour_index,
    neighbour_count,
    edge_weight,
    cotangent,
):
    channels, step_count, sensor_count = signal.shape
    row_count = channels * step_count
    slot_count = neighbour_index.shape[1]
    peer_count = lax.axis_size("sensor")
    myself = lax.axis_index("sensor")
    owner = neighbour_index // sensor_count
    member = neighbour_index % sensor_count
    live = lax.broadcasted_iota(jnp.int32, (sensor_count, slot_count), 1) < neighbour_count[:, None]
    distant = live & (owner != myself)
    masked = jnp.where(live, edge_weight, 0.0)
    trans = (masked / jnp.sum(masked, axis=1, keepdims=True)).astype(jnp.bfloat16)
    row_ids = lax.broadcasted_iota(jnp.int32, (sensor_count, slot_count), 0)
    wanted = (
        jnp.zeros((peer_count, sensor_count), jnp.int32)
        .at[owner, member]
        .max(distant.astype(jnp.int32))
    )
    wanted_slot, requests = compact_list(wanted, peer_count, sensor_count)
    columns = jnp.where(
        distant, sensor_count + owner * CAPACITY + wanted_slot[owner, member], member
    )
    table = jnp.zeros((sensor_count, sensor_count + peer_count * CAPACITY), jnp.float32)
    table = table.at[row_ids, columns].add(trans.astype(jnp.float32))
    near_table = table[:, :sensor_count].astype(jnp.bfloat16)
    far_table = table[:, sensor_count:].astype(jnp.bfloat16)
    contract_rows = (((1,), (1,)), ((), ()))
    send_list = lax.all_to_all(requests, "sensor", split_axis=0, concat_axis=0, tiled=True)
    sensor_ids = lax.broadcasted_iota(jnp.int32, (peer_count * CAPACITY, sensor_count), 1)
    one_hot = (send_list.reshape(-1)[:, None] == sensor_ids).astype(jnp.float32)

    def absorb_back(pieces):
        flat = pieces.reshape(pieces.shape[0], peer_count * CAPACITY)
        return jnp.dot(
            flat, one_hot, precision=lax.Precision.HIGHEST, preferred_element_type=jnp.float32
        )

    def spread_back(values):
        own_part = jnp.dot(values, near_table, preferred_element_type=jnp.float32)
        terms = jnp.dot(values, far_table, preferred_element_type=jnp.float32).reshape(
            row_count, peer_count, CAPACITY
        )
        return own_part + absorb_back(
            lax.all_to_all(terms, "sensor", split_axis=1, concat_axis=1, tiled=True)
        )

    send_index = jnp.maximum(send_list, 0).reshape(-1)

    def absorb(pieces):
        flat = pieces.reshape(pieces.shape[0], peer_count * CAPACITY)
        return lax.dot_general(flat, far_table, contract_rows, preferred_element_type=jnp.float32)

    def spread(values):
        own_part = lax.dot_general(
            values, near_table, contract_rows, preferred_element_type=jnp.float32
        )
        outgoing = jnp.take(values, send_index, axis=1).reshape(row_count, peer_count, CAPACITY)
        return own_part + absorb(
            lax.all_to_all(outgoing, "sensor", split_axis=1, concat_axis=1, tiled=True)
        )

    tail_steps = signal[:, step_count - DILATION :, :]
    before = from_behind(tail_steps, "tm", 1)
    lagged = jnp.concatenate([before, signal[:, : step_count - DILATION, :]], axis=1)
    stacked = jnp.concatenate([lagged, signal], axis=0).reshape(
        2 * channels, step_count * sensor_count
    )
    preact = jnp.dot(conv_weight, stacked, preferred_element_type=jnp.float32) + conv_bias[:, None]
    tanh_part = jnp.tanh(preact[:channels])
    gate_part = jax.nn.sigmoid(preact[channels:])
    hidden = (tanh_part * gate_part).astype(jnp.bfloat16)
    hop_one = spread(hidden.reshape(row_count, sensor_count)).astype(jnp.bfloat16)
    hop_two = spread(hop_one).astype(jnp.bfloat16)
    joined = jnp.concatenate(
        [hidden, hop_one.reshape(channels, -1), hop_two.reshape(channels, -1)], axis=0
    )
    mixed = jnp.dot(diff_weight, joined, preferred_element_type=jnp.float32)
    output = (signal.reshape(channels, -1).astype(jnp.float32) + mixed).astype(jnp.bfloat16)
    output = output.reshape(channels, step_count, sensor_count)
    grad_flat = cotangent.reshape(channels, step_count * sensor_count)
    theta_back = lax.dot_general(
        diff_weight, grad_flat, (((0,), (0,)), ((), ())), preferred_element_type=jnp.float32
    )
    second = theta_back[2 * channels :].astype(jnp.bfloat16).reshape(row_count, sensor_count)
    first = theta_back[channels : 2 * channels] + spread_back(second).reshape(channels, -1)
    first = first.astype(jnp.bfloat16).reshape(row_count, sensor_count)
    grad_hidden = theta_back[:channels] + spread_back(first).reshape(channels, -1)
    grad_tanh = grad_hidden * gate_part * (1.0 - tanh_part * tanh_part)
    grad_gate = grad_hidden * tanh_part * gate_part * (1.0 - gate_part)
    grad_pre = jnp.concatenate([grad_tanh, grad_gate], axis=0).astype(jnp.bfloat16)
    conv_back = lax.dot_general(
        conv_weight, grad_pre, (((0,), (0,)), ((), ())), preferred_element_type=jnp.float32
    )
    lag_back = conv_back[:channels].reshape(channels, step_count, sensor_count)
    now_back = conv_back[channels:].reshape(channels, step_count, sensor_count)
    after = from_behind(lag_back[:, :DILATION, :].astype(jnp.bfloat16), "tm", -1).astype(
        jnp.float32
    )
    shifted = jnp.concatenate([lag_back[:, DILATION:, :], after], axis=1)
    grad_signal = (cotangent.astype(jnp.float32) + now_back + shifted).astype(jnp.bfloat16)
    return (output, grad_signal)


def solution(mesh):
    placed = (
        P(None, "tm", "sensor"),
        P(),
        P(),
        P(),
        P("sensor", None),
        P("sensor"),
        P("sensor", None),
        P(None, "tm", "sensor"),
    )
    return jax.shard_map(
        per_device,
        mesh=mesh,
        in_specs=placed,
        out_specs=(P(None, "tm", "sensor"), P(None, "tm", "sensor")),
        check_vma=False,
    )
```

profile of v0, /device:TPU:6, one launch (start us, length us, event | category | flops | bytes accessed | tf_op | source)
XLA Modules:
  0.0 845.6 jit_solution(16189996439217850070)
XLA Ops:
  0.6 0.7 fusion.46
  1.4 0.7 multiply_reduce_fusion.2
  2.1 0.7 and_reduce_fusion.2
  3.0 0.8 fusion.55
  4.0 27.5 %scatter_custom_fusion = s32[8192]{0:T(1024)S(1)} fusion(s32[4096]{0:T(1024)S(1)} %reshape.157, s32[4096]{0:T(1024)S(1)} %reshape.159, s32[]{:T(128)} %constant.62.clone.1), kind=kCustom, calls=%fused_computation.98 | custom fusion | flops 4096 | bytes 32772
  31.8 0.7 multiply_reduce_fusion
  32.5 0.7 and_reduce_fusion
  33.3 30.4 %scatter_custom_fusion.2 = s32[256]{0:T(256)S(1)} fusion(s32[8192]{0:T(1024)S(1)} %get-tuple-element.12, s32[8192]{0:T(1024)S(1)} %get-tuple-element.13, s32[]{:T(128)} %constant.65.clone.1), kind=kCustom, calls=%fused_computation.115 | custom fusion | bytes 1028
  63.8 0.7 copy.58
  64.5 18.8 %all-to-all-start = ((s32[64,1,4]{2,1,0:T(1,128)}), s32[64,1,4]{2,1,0:T(1,128)S(1)}, u32[]{:S(2)}, u32[]{:S(2)}) async-start(s32[64,1,4]{2,1,0:T(1,128)} %copy.58), calls=%async_computation | async-start | bytes 65536 | tf_op jit(solution)/shard_map/all_to_all | solution.py:63
  83.3 0.7 shift-left_or_fusion
  84.3 25.6 %gather_fusion = s32[4096]{0:T(1024)S(1)} fusion(s32[64,128]{1,0:T(8,128)S(1)} %get-tuple-element.9, s32[4096]{0:T(1024)S(1)} %reshape.151), kind=kCustom, calls=%fused_computation.2 | custom fusion | bytes 65536 | tf_op jit(solution)/shard_map/gather | solution.py:56
  110.7 28.5 %scatter_custom_fusion.1 = f32[49152]{0:T(1024)S(1)} fusion(s32[4096]{0:T(1024)S(1)} %reshape.163, f32[4096]{0:T(1024)S(1)} %reshape.165, f32[]{:T(128)} %constant.60.clone.1), kind=kCustom, calls=%fused_computation.54 | custom fusion | flops 4096 | bytes 196612
  139.4 1.0 fusion.24
  140.5 2.6 copy-done.1
  143.8 0.7 fusion.33
  144.5 4.8 copy.63
  149.3 15.8 %all-to-all-start.3 = ((f32[4096,64,4]{0,2,1:T(4,128)}), f32[4096,64,4]{0,2,1:T(4,128)}, u32[]{:S(2)}, u32[]{:S(2)}) async-start(f32[4096,64,4]{0,2,1:T(4,128)} %copy.63), calls=%async_computation.3 | async-start | bytes 8388608 | tf_op jit(solution)/shard_map/all_to_all | solution.py:79
  166.6 0.7 reduce.15
  167.4 187.1 %all-to-all-done.3 = f32[4096,64,4]{0,2,1:T(4,128)} async-done(((f32[4096,64,4]{0,2,1:T(4,128)}), f32[4096,64,4]{0,2,1:T(4,128)}, u32[]{:S(2)}, u32[]{:S(2)}) %all-to-all-start.3) | async-done | bytes 4194336 | tf_op jit(solution)/shard_map/all_to_all | solution.py:79
  354.5 5.3 reshape.114
  359.7 7.0 convolution_add_fusion.2
  366.8 1.7 reshape.115
  368.5 1.8 fusion.14
  370.8 0.7 fusion.31
  371.6 4.7 copy.65
  376.2 6.2 all-to-all-start.4
  382.5 2.2 collective-permute-start
  384.8 4.1 collective-permute-done
  389.3 3.7 fusion
  393.0 1.3 reshape.116
  394.3 1.6 fusion.38
  395.9 175.7 %all-to-all-done.4 = f32[4096,64,4]{0,2,1:T(4,128)} async-done(((f32[4096,64,4]{0,2,1:T(4,128)}), f32[4096,64,4]{0,2,1:T(4,128)}, u32[]{:S(2)}, u32[]{:S(2)}) %all-to-all-start.4) | async-done | bytes 4194336 | tf_op jit(solution)/shard_map/all_to_all | solution.py:79
  571.7 5.3 reshape.117
  577.0 7.0 convolution_add_fusion.1
  584.0 1.7 reshape.118
  585.7 5.5 multiply_convert_fusion.1
  591.2 1.6 reshape.104
  592.8 0.5 copy.59
  593.3 3.2 gather_fusion.1
  596.5 3.2 select_bitcast_fusion.1
  599.7 4.1 reshape.105
  603.8 6.3 all-to-all-start.1
  610.1 1.7 fusion.44
  611.9 97.5 %all-to-all-done.1 = bf16[4096,64,4]{0,2,1:T(4,128)(2,1)} async-done(((bf16[4096,64,4]{0,2,1:T(4,128)(2,1)}), bf16[4096,64,4]{0,2,1:T(4,128)(2,1)}, u32[]{:S(2)}, u32[]{:S(2)}) %all-to-all-start.1) | async-done | bytes 2097184 | tf_op jit(solution)/shard_map/all_to_all | solution.py:94
  709.4 4.0 reshape.106
  713.3 3.0 fusion.3
  716.9 3.2 gather_fusion.2
  720.1 3.2 select_bitcast_fusion
  723.3 4.1 reshape.108
  727.4 6.2 all-to-all-start.2
  733.6 2.0 convolution_bitcast_fusion
  736.4 1.9 collective-permute-start.1
  738.3 1.6 convert.29
  741.3 1.4 fusion.11
  742.7 1.3 reshape.107
  744.1 1.8 fusion.42
  745.8 86.4 %all-to-all-done.2 = bf16[4096,64,4]{0,2,1:T(4,128)(2,1)} async-done(((bf16[4096,64,4]{0,2,1:T(4,128)(2,1)}), bf16[4096,64,4]{0,2,1:T(4,128)(2,1)}, u32[]{:S(2)}, u32[]{:S(2)}) %all-to-all-start.2) | async-done | bytes 2097184 | tf_op jit(solution)/shard_map/all_to_all | solution.py:94
  832.3 4.0 reshape.109
  836.2 2.3 fusion.4
  838.6 1.3 reshape.110
  839.9 0.6 copy-done.8
  840.5 3.6 fusion.21
  844.2 1.3 copy.68
  (82 shorter events, 7.7 us)
Async XLA Ops:
  0.6 388.6 %copy-start = (bf16[128,128]{1,0:T(8,128)(2,1)S(1)}, bf16[128,128]{1,0:T(8,128)(2,1)}, u32[]{:S(2)}) copy-start(bf16[128,128]{1,0:T(8,128)(2,1)} %param.11) | copy-start | bytes 98308
  64.5 84.7 %all-to-all-start = ((s32[64,1,4]{2,1,0:T(1,128)}), s32[64,1,4]{2,1,0:T(1,128)S(1)}, u32[]{:S(2)}, u32[]{:S(2)}) async-start(s32[64,1,4]{2,1,0:T(1,128)} %copy.58), calls=%async_computation | async-start | bytes 65536 | tf_op jit(solution)/shard_map/all_to_all | solution.py:63
  84.2 25.8 %copy-start.9 = (s32[128,32]{0,1:T(8,128)S(1)}, s32[128,32]{0,1:T(8,128)}, u32[]{:S(2)}) copy-start(s32[128,32]{0,1:T(8,128)} %param.14) | copy-start | bytes 49156
  84.2 25.8 %copy-start.12 = (s32[128]{0:T(128)S(1)}, s32[128]{0:T(128)}, u32[]{:S(2)}) copy-start(s32[128]{0:T(128)} %param.15) | copy-start | bytes 1540
  84.3 25.9 %copy-start.15 = (s32[2]{0:T(128)S(1)}, s32[2]{0:T(128)}, u32[]{:S(2)}) copy-start(s32[2]{0:T(128)} %constant.78) | copy-start | bytes 28
  84.3 26.0 %copy-start.14 = (s32[2]{0:T(128)S(1)}, s32[2]{0:T(128)}, u32[]{:S(2)}) copy-start(s32[2]{0:T(128)} %constant.81) | copy-start | bytes 28
  84.3 26.2 %copy-start.10 = (f32[128,32]{0,1:T(8,128)S(1)}, f32[128,32]{0,1:T(8,128)}, u32[]{:S(2)}) copy-start(f32[128,32]{0,1:T(8,128)} %param.16) | copy-start | bytes 49156
  84.3 55.1 %copy-start.11 = (bf16[64,192]{1,0:T(8,128)(2,1)S(1)}, bf16[64,192]{1,0:T(8,128)(2,1)}, u32[]{:S(2)}) copy-start(bf16[64,192]{1,0:T(8,128)(2,1)} %param.13) | copy-start | bytes 73732
  109.9 29.5 %copy-start.4 = (bf16[64,64,128]{2,1,0:T(8,128)(2,1)S(1)}, bf16[64,64,128]{2,1,0:T(8,128)(2,1)}, u32[]{:S(2)}) copy-start(bf16[64,64,128]{2,1,0:T(8,128)(2,1)} %param.17) | copy-start | bytes 3145732
  140.5 2.7 copy-start.1
  149.3 205.2 %all-to-all-start.3 = ((f32[4096,64,4]{0,2,1:T(4,128)}), f32[4096,64,4]{0,2,1:T(4,128)}, u32[]{:S(2)}, u32[]{:S(2)}) async-start(f32[4096,64,4]{0,2,1:T(4,128)} %copy.63), calls=%async_computation.3 | async-start | bytes 8388608 | tf_op jit(solution)/shard_map/all_to_all | solution.py:79
  376.2 6.2 copy-start.2
  376.2 195.4 %all-to-all-start.4 = ((f32[4096,64,4]{0,2,1:T(4,128)}), f32[4096,64,4]{0,2,1:T(4,128)}, u32[]{:S(2)}, u32[]{:S(2)}) async-start(f32[4096,64,4]{0,2,1:T(4,128)} %copy.65), calls=%async_computation.4 | async-start | bytes 8388608 | tf_op jit(solution)/shard_map/all_to_all | solution.py:79
  382.5 6.5 slice-start
  382.5 6.4 collective-permute-start
  384.8 4.5 copy-start.13
  603.8 105.6 %all-to-all-start.1 = ((bf16[4096,64,4]{0,2,1:T(4,128)(2,1)}), bf16[4096,64,4]{0,2,1:T(4,128)(2,1)}, u32[]{:S(2)}, u32[]{:S(2)}) async-start(bf16[4096,64,4]{0,2,1:T(4,128)(2,1)} %reshape.105), calls=%async_computation.1 | async-start | bytes 4194304 | tf_op jit(solution)/shard_map/all_to_all | solution.py:94
  727.4 6.2 copy-start.6
  727.4 104.9 %all-to-all-start.2 = ((bf16[4096,64,4]{0,2,1:T(4,128)(2,1)}), bf16[4096,64,4]{0,2,1:T(4,128)(2,1)}, u32[]{:S(2)}, u32[]{:S(2)}) async-start(bf16[4096,64,4]{0,2,1:T(4,128)(2,1)} %reshape.108), calls=%async_computation.2 | async-start | bytes 4194304 | tf_op jit(solution)/shard_map/all_to_all | solution.py:94
  736.4 4.4 collective-permute-start.1
  740.1 1.2 copy-start.5
  745.8 90.4 %copy-start.3 = (f32[4096,128]{1,0:T(8,128)S(1)}, f32[4096,128]{1,0:T(8,128)}, u32[]{:S(2)}) copy-start(f32[4096,128]{1,0:T(8,128)} %fusion.42) | copy-start | bytes 6291460
  838.6 1.3 copy-start.7
  838.6 1.9 copy-start.8
where the time goes:
time: 856 us; the launch traced here: 846 us
  waiting for transfers between devices  551 us (64%)
  local copies, waits for them, and re-layouts  119 us (14%)
  other arithmetic  79.4 us (9%)
  starting transfers between devices  57.5 us (7%)
  matrix products  36.7 us (4%)
    all_to_all x2, waiting for transfers between devices, spread_back(): lax.all_to_all(terms, 'sensor', split_axis=1, concat_axis=1, tiled=True)  363 us
    all_to_all x2, waiting for transfers between devices, spread(): lax.all_to_all(outgoing, 'sensor', split_axis=1, concat_axis=1, tiled=True)  184 us
    unnamed x12, other arithmetic  60.7 us
    unnamed x42, local copies, waits for them, and re-layouts  37.1 us
    gather x3, local copies, waits for them, and re-layouts, per_device(): wanted_slot[owner, member]  25.7 us
    all_to_all x2, starting transfers between devices, spread_back(): lax.all_to_all(terms, 'sensor', split_axis=1, concat_axis=1, tiled=True)  22.1 us
    all_to_all x1, starting transfers between devices, per_device(): lax.all_to_all(requests, 'sensor', split_axis=0, concat_axis=0, tiled=True)  18.8 us
  transfers between devices with their start and end apart: 7, of which 6 were waited for; matrix products, arithmetic and copies ran while one was open for 10% of the time, Pallas kernels for 0%

commit v1 on v0

v1 whole, which is shorter than its diff:
```python
import functools

import jax
import jax.numpy as jnp
from jax import lax
from jax.experimental import pallas as pl
from jax.experimental.pallas import tpu as pltpu
from jax.sharding import PartitionSpec as P

DILATION = 8
CAPACITY = 4

ROWS_BY_ROWS = (((1,), (1,)), ((), ()))


def from_behind(value, axis, by):
    count = lax.axis_size(axis)
    pairs = [(i, i + by) for i in range(count) if 0 <= i + by < count]
    return lax.ppermute(value, axis, pairs)


def mm(left, right):
    return jnp.dot(left, right, preferred_element_type=jnp.float32)


def mm_t(left, right):
    return lax.dot_general(left, right, ROWS_BY_ROWS, preferred_element_type=jnp.float32)


def table_kernel(peers, me_ref, index_ref, count_ref, weight_ref, near_ref, far_ref, request_ref, member_all, owner_all):
    sensors, slots = index_ref.shape
    me = me_ref[0]
    index = index_ref[...].T
    live = lax.broadcasted_iota(jnp.int32, (slots, sensors), 0) < count_ref[...]
    masked = jnp.where(live, weight_ref[...].T, 0.0)
    trans = masked / jnp.sum(masked, axis=0, keepdims=True)
    trans = trans.astype(jnp.bfloat16).astype(jnp.float32)
    owner = jnp.where(live, index // sensors, -1)
    member = index % sensors
    member_ids = lax.broadcasted_iota(jnp.int32, (sensors, sensors), 0)
    owner_ids = lax.broadcasted_iota(jnp.int32, (peers, sensors), 0)
    near = jnp.zeros((sensors, sensors), jnp.float32)
    for j in range(slots):
        place = slice(j * sensors, (j + 1) * sensors)
        hit = member_ids == member[j : j + 1]
        member_all[:, place] = jnp.where(hit, 1.0, 0.0).astype(jnp.bfloat16)
        owner_all[:, place] = jnp.where(owner_ids == owner[j : j + 1], 1.0, 0.0).astype(jnp.bfloat16)
        home = jnp.where(owner[j : j + 1] == me, trans[j : j + 1], 0.0)
        near = near + jnp.where(hit, home, 0.0)
    near_ref[...] = near.astype(jnp.bfloat16)
    named = mm_t(owner_all[...], member_all[...])
    named = (named > 0.0) & (owner_ids != me)
    flags = jnp.where(named, 1.0, 0.0).astype(jnp.bfloat16)
    below = lax.broadcasted_iota(jnp.int32, (sensors, sensors), 0) < lax.broadcasted_iota(
        jnp.int32, (sensors, sensors), 1
    )
    rank = mm(flags, jnp.where(below, 1.0, 0.0).astype(jnp.bfloat16))
    rank = jnp.where(named, rank, 255.0).astype(jnp.bfloat16)
    places = peers * CAPACITY
    expand = lax.broadcasted_iota(jnp.int32, (places, peers), 0) // CAPACITY == lax.broadcasted_iota(
        jnp.int32, (places, peers), 1
    )
    rank = mm(jnp.where(expand, 1.0, 0.0).astype(jnp.bfloat16), rank)
    place_ids = lax.broadcasted_iota(jnp.int32, (places, sensors), 0)
    wanted_rank = (place_ids % CAPACITY).astype(jnp.float32)
    chosen = jnp.where(rank == wanted_rank, 1.0, 0.0).astype(jnp.bfloat16)
    lane_ids = lax.broadcasted_iota(jnp.int32, (8, sensors), 1).astype(jnp.float32)
    label = jnp.where(lax.broadcasted_iota(jnp.int32, (8, sensors), 0) == 0, lane_ids, 1.0).astype(jnp.bfloat16)
    asked = mm_t(label, chosen).astype(jnp.int32)
    request_ref[...] = jnp.where(asked[1:2] > 0, asked[0:1], -1)
    place_owner = place_ids // CAPACITY
    far = jnp.zeros((places, sensors), jnp.float32)
    for j in range(slots):
        found = mm(chosen, member_all[:, j * sensors : (j + 1) * sensors])
        far = far + jnp.where(place_owner == owner[j : j + 1], found * trans[j : j + 1], 0.0)
    far_ref[...] = far.astype(jnp.bfloat16)


def swap_requests(request, axis):
    count = lax.axis_size(axis)
    me = lax.axis_index(axis)
    width = request.shape[1]
    blocks = lax.dynamic_slice_in_dim(jnp.concatenate([request, request], axis=0), me, count, 0)
    step = 1
    while step < count:
        parts = blocks.reshape(count // (2 * step), 2, step * width)
        moved = lax.ppermute(parts[:, 1], axis, [(i, (i + step) % count) for i in range(count)])
        blocks = jnp.stack([parts[:, 0], moved], axis=1).reshape(count, width)
        step *= 2
    blocks = jnp.concatenate([blocks[:1], blocks[:0:-1]], axis=0)
    return lax.dynamic_slice_in_dim(jnp.concatenate([blocks, blocks], axis=0), count - me, count, 0)


def build_tables(peers, myself, index, count, weight):
    sensors, slots = index.shape
    places = peers * CAPACITY
    vmem = pl.BlockSpec(memory_space=pltpu.VMEM)
    return pl.pallas_call(
        functools.partial(table_kernel, peers),
        out_shape=(
            jax.ShapeDtypeStruct((sensors, sensors), jnp.bfloat16),
            jax.ShapeDtypeStruct((places, sensors), jnp.bfloat16),
            jax.ShapeDtypeStruct((1, places), jnp.int32),
        ),
        in_specs=[pl.BlockSpec(memory_space=pltpu.SMEM), vmem, vmem, vmem],
        out_specs=(vmem, vmem, vmem),
        scratch_shapes=[
            pltpu.VMEM((sensors, slots * sensors), jnp.bfloat16),
            pltpu.VMEM((peers, slots * sensors), jnp.bfloat16),
        ],
        compiler_params=pltpu.CompilerParams(vmem_limit_bytes=32 * 1024 * 1024),
        cost_estimate=pl.CostEstimate(flops=4 * 10**8, bytes_accessed=10**6, transcendentals=0),
        name="tables",
    )(myself.reshape(1).astype(jnp.int32), index, count.reshape(1, sensors), weight)


def per_device(
    signal,
    conv_weight,
    conv_bias,
    diff_weight,
    neighbour_index,
    neighbour_count,
    edge_weight,
    cotangent,
):
    channels, step_count, sensor_count = signal.shape
    row_count = channels * step_count
    peer_count = lax.axis_size("sensor")
    myself = lax.axis_index("sensor")
    near_t, far_t, request = build_tables(
        peer_count, myself, neighbour_index, neighbour_count, edge_weight
    )

    def exchange(pieces, earlier=None):
        shaped = pieces.astype(jnp.bfloat16).reshape(peer_count, CAPACITY, row_count)
        if earlier is not None:
            shaped, earlier = lax.optimization_barrier((shaped, earlier))
        return lax.all_to_all(shaped, "sensor", split_axis=0, concat_axis=0, tiled=True)

    def absorb(arrived, places):
        return lax.dot_general(
            arrived.reshape(peer_count * CAPACITY, row_count),
            places,
            (((0,), (0,)), ((), ())),
            preferred_element_type=jnp.float32,
        )

    grad_flat = cotangent.reshape(channels, step_count * sensor_count)
    theta_back = lax.dot_general(
        diff_weight, grad_flat, (((0,), (0,)), ((), ())), preferred_element_type=jnp.float32
    )
    second = theta_back[2 * channels :].astype(jnp.bfloat16).reshape(row_count, sensor_count)
    second_far = exchange(mm_t(far_t, second))

    asked = swap_requests(request.reshape(peer_count, CAPACITY), "sensor")
    pick = (asked[:, :, None] == lax.broadcasted_iota(jnp.int32, (1, 1, sensor_count), 2)).astype(jnp.bfloat16)
    pick = lax.optimization_barrier(pick.reshape(peer_count * CAPACITY, sensor_count))

    tail_steps = signal[:, step_count - DILATION :, :]
    before = from_behind(tail_steps, "tm", 1)
    lagged = jnp.concatenate([before, signal[:, : step_count - DILATION, :]], axis=1)
    stacked = jnp.concatenate([lagged, signal], axis=0).reshape(
        2 * channels, step_count * sensor_count
    )
    preact = mm(conv_weight, stacked) + conv_bias[:, None]
    tanh_part = jnp.tanh(preact[:channels])
    gate_part = jax.nn.sigmoid(preact[channels:])
    hidden = (tanh_part * gate_part).astype(jnp.bfloat16)
    hidden_rows = hidden.reshape(row_count, sensor_count)
    hidden_far = exchange(mm_t(pick, hidden_rows), second_far)

    first = theta_back[channels : 2 * channels] + (
        mm_t(second, near_t) + absorb(second_far, pick)
    ).reshape(channels, -1)
    first = first.astype(jnp.bfloat16).reshape(row_count, sensor_count)
    first_far = exchange(mm_t(far_t, first), hidden_far)

    hop_one = (mm(hidden_rows, near_t) + absorb(hidden_far, far_t)).astype(jnp.bfloat16)
    hop_far = exchange(mm_t(pick, hop_one), first_far)

    grad_hidden = theta_back[:channels] + (
        mm_t(first, near_t) + absorb(first_far, pick)
    ).reshape(channels, -1)
    grad_tanh = grad_hidden * gate_part * (1.0 - tanh_part * tanh_part)
    grad_gate = grad_hidden * tanh_part * gate_part * (1.0 - gate_part)
    grad_pre = jnp.concatenate([grad_tanh, grad_gate], axis=0).astype(jnp.bfloat16)
    conv_back = lax.dot_general(
        conv_weight, grad_pre, (((0,), (0,)), ((), ())), preferred_element_type=jnp.float32
    )
    lag_back = conv_back[:channels].reshape(channels, step_count, sensor_count)
    now_back = conv_back[channels:].reshape(channels, step_count, sensor_count)
    after = from_behind(lag_back[:, :DILATION, :].astype(jnp.bfloat16), "tm", -1).astype(
        jnp.float32
    )
    shifted = jnp.concatenate([lag_back[:, DILATION:, :], after], axis=1)
    grad_signal = (cotangent.astype(jnp.float32) + now_back + shifted).astype(jnp.bfloat16)

    hop_two = (mm(hop_one, near_t) + absorb(hop_far, far_t)).astype(jnp.bfloat16)
    joined = jnp.concatenate(
        [hidden, hop_one.reshape(channels, -1), hop_two.reshape(channels, -1)], axis=0
    )
    mixed = mm(diff_weight, joined)
    output = (signal.reshape(channels, -1).astype(jnp.float32) + mixed).astype(jnp.bfloat16)
    output = output.reshape(channels, step_count, sensor_count)
    return (output, grad_signal)


def solution(mesh):
    placed = (
        P(None, "tm", "sensor"),
        P(),
        P(),
        P(),
        P("sensor", None),
        P("sensor"),
        P("sensor", None),
        P(None, "tm", "sensor"),
    )
    return jax.shard_map(
        per_device,
        mesh=mesh,
        in_specs=placed,
        out_specs=(P(None, "tm", "sensor"), P(None, "tm", "sensor")),
        check_vma=False,
    )
```

time: 856 us -> 515 us (0.60)
  waiting for transfers between devices: 551 us -> 324 us
  other arithmetic: 79.4 us -> 11.5 us
  local copies, waits for them, and re-layouts: 119 us -> 56.6 us
  starting transfers between devices: 57.5 us -> 77.4 us
    all_to_all x5 -> x4, waiting for transfers between devices: 547 us -> 216 us  [exchange(): lax.all_to_all(shaped, 'sensor', split_axis=0, concat_axis=0, tiled=True)]
    ppermute x0 -> x6, waiting for transfers between devices: none -> 104 us  [swap_requests(): lax.ppermute(parts[:, 1], axis, [(i, (i + step) % count) for i in range(c...]
    unnamed x12 -> x1, other arithmetic: 60.7 us -> 1.61 us
    gather x5 -> x0, local copies, waits for them, and re-layouts: 32.1 us -> none  [the longest x3 25.7 us: per_device(): wanted_slot[owner, member]]
    ppermute x0 -> x6, starting transfers between devices: none -> 31.5 us  [swap_requests(): lax.ppermute(parts[:, 1], axis, [(i, (i + step) % count) for i in range(c...]
    unnamed x42 -> x36, local copies, waits for them, and re-layouts: 37.1 us -> 12.7 us
    all_to_all x5 -> x4, starting transfers between devices: 53.4 us -> 41.1 us  [exchange(): lax.all_to_all(shaped, 'sensor', split_axis=0, concat_axis=0, tiled=True)]
    dot_general x4 -> x0, local copies, waits for them, and re-layouts: 9.56 us -> none  [spread_back(): jnp.dot(values, far_table, preferred_element_type=jnp.float32)]
  transfers between devices with their start and end apart: 7 -> 12, of which waited for: 6 -> 9; matrix products, arithmetic and copies ran while one was open for 10% -> 15% of each run, Pallas kernels for 0% -> 0%
where the time goes in v1:
time: 515 us; the launch traced here: 508 us
  waiting for transfers between devices  324 us (63%)
  starting transfers between devices  77.4 us (15%)
  local copies, waits for them, and re-layouts  56.6 us (11%)
  matrix products  35.1 us (7%)
  other arithmetic  11.5 us (2%)
    all_to_all x4, waiting for transfers between devices, exchange(): lax.all_to_all(shaped, 'sensor', split_axis=0, concat_axis=0, tiled=True)  216 us
    ppermute x6, waiting for transfers between devices, swap_requests(): lax.ppermute(parts[:, 1], axis, [(i, (i + step) % count) for i in range(c...  104 us
    all_to_all x4, starting transfers between devices, exchange(): lax.all_to_all(shaped, 'sensor', split_axis=0, concat_axis=0, tiled=True)  41.1 us
    ppermute x6, starting transfers between devices, swap_requests(): lax.ppermute(parts[:, 1], axis, [(i, (i + step) % count) for i in range(c...  31.5 us
    reshape x4, local copies, waits for them, and re-layouts, absorb(): arrived.reshape(peer_count * CAPACITY, row_count)  16 us
    reshape x4, local copies, waits for them, and re-layouts, exchange(): pieces.astype(jnp.bfloat16).reshape(peer_count, CAPACITY, row_count)  14.6 us
    dot_general x4, matrix products, absorb(): lax.dot_general(arrived.reshape(peer_count * CAPACITY, row_count), places...  14.4 us
    unnamed x36, local copies, waits for them, and re-layouts  12.7 us
  transfers between devices with their start and end apart: 12, of which 9 were waited for; matrix products, arithmetic and copies ran while one was open for 15% of the time, Pallas kernels for 0%

profile of v1, /device:TPU:6, one launch (start us, length us, event | category | flops | bytes accessed | tf_op | source)
XLA Modules:
  0.0 507.8 jit_solution(10363069506584922281)
XLA Ops:
  0.6 0.8 copy.43.index_ref
  1.5 0.8 copy.44.weight_ref
  2.3 2.3 fusion.24
  4.6 2.6 copy-done.3
  7.9 2.2 tables.1
  10.0 0.7 convolution_convert_fusion.2
  10.7 2.2 reshape.97
  13.0 19.1 %all-to-all-start = ((bf16[64,4,4096]{2,1,0:T(4,128)(2,1)}), bf16[64,4,4096]{2,1,0:T(4,128)(2,1)}, u32[]{:S(2)}, u32[]{:S(2)}) async-start(bf16[64,4,4096]{2,1,0:T(4,128)(2,1)} %reshape.97), calls=%async_computation | async-start | bytes 4194304 | tf_op jit(solution)/shard_map/all_to_all | solution.py:139
  32.6 0.7 reduce.3
  33.9 3.4 collective-permute-start.1
  37.3 85.1 %collective-permute-done.1 = s32[32,4]{0,1:T(4,128)S(1)} collective-permute-done((s32[32,4]{0,1:T(4,128)S(1)}, s32[32,4]{0,1:T(4,128)S(1)}, u32[]{:S(2)}, u32[]{:S(2)}) %collective-permute-start.1) | collective-permute-done | bytes 544 | tf_op jit(solution)/shard_map/ppermute | solution.py:87
  122.7 1.9 collective-permute-start.2
  124.6 7.2 %collective-permute-done.2 = s32[16,8]{0,1:T(8,128)S(1)} collective-permute-done((s32[16,8]{0,1:T(8,128)S(1)}, s32[16,8]{0,1:T(8,128)S(1)}, u32[]{:S(2)}, u32[]{:S(2)}) %collective-permute-start.2) | collective-permute-done | bytes 544 | tf_op jit(solution)/shard_map/ppermute | solution.py:87
  132.0 1.9 collective-permute-start.3
  133.9 5.0 collective-permute-done.3
  139.0 2.1 collective-permute-start.4
  141.1 5.5 %collective-permute-done.4 = s32[4,32]{1,0:T(4,128)S(1)} collective-permute-done((s32[4,32]{1,0:T(4,128)S(1)}, s32[4,32]{1,0:T(4,128)S(1)}, u32[]{:S(2)}, u32[]{:S(2)}) %collective-permute-start.4) | collective-permute-done | bytes 544 | tf_op jit(solution)/shard_map/ppermute | solution.py:87
  146.7 8.6 %collective-permute-start.5 = (s32[2,64]{1,0:T(2,128)S(1)}, s32[2,64]{1,0:T(2,128)S(1)}, u32[]{:S(2)}, u32[]{:S(2)}) collective-permute-start(s32[2,64]{1,0:T(2,128)S(1)} %bitcast.106), channel_id=1, source_target_pairs={{0,128},{8,136},{16,144},{24,152},{32,160},{40,168},{48,176},{56,1... | collective-permute-start | bytes 1544 | tf_op jit(solution)/shard_map/ppermute | solution.py:87
  155.3 1.3 collective-permute-done.5
  156.6 13.6 %collective-permute-start.6 = (s32[1,128]{1,0:T(1,128)S(1)}, s32[1,128]{1,0:T(1,128)S(1)}, u32[]{:S(2)}, u32[]{:S(2)}) collective-permute-start(s32[1,128]{1,0:T(1,128)S(1)} %get-tuple-element.29), channel_id=1, source_target_pairs={{0,256},{8,264},{16,272},{24,280},{32,288},{40,296},{48,304},{56,3... | collective-permute-start | bytes 1544 | tf_op jit(solution)/shard_map/ppermute | solution.py:87
  170.4 1.9 collective-permute-start
  173.1 3.5 collective-permute-done
  177.0 1.7 fusion
  178.7 2.1 copy-done.2
  180.8 0.8 multiply_convert_fusion.2
  182.2 2.1 convolution_convert_fusion.3
  184.2 4.1 reshape.94
  188.4 9.7 %all-to-all-start.1 = ((bf16[64,4,4096]{2,1,0:T(4,128)(2,1)}), bf16[64,4,4096]{2,1,0:T(4,128)(2,1)}, u32[]{:S(2)}, u32[]{:S(2)}) async-start(bf16[64,4,4096]{2,1,0:T(4,128)(2,1)} %reshape.94), calls=%async_computation.1 | async-start | bytes 4194304 | tf_op jit(solution)/shard_map/all_to_all | solution.py:139
  198.1 1.8 fusion.38
  199.9 3.9 reshape.101
  203.8 4.3 convolution_add_fusion.3
  208.1 2.7 reshape.102
  210.9 2.4 fusion.14
  213.8 2.1 convolution_convert_fusion
  215.9 4.1 reshape.104
  220.0 71.4 %all-to-all-done.1 = bf16[64,4,4096]{2,1,0:T(4,128)(2,1)} async-done(((bf16[64,4,4096]{2,1,0:T(4,128)(2,1)}), bf16[64,4,4096]{2,1,0:T(4,128)(2,1)}, u32[]{:S(2)}, u32[]{:S(2)}) %all-to-all-start.1) | async-done | bytes 2097184 | tf_op jit(solution)/shard_map/all_to_all | solution.py:139
  291.4 6.1 %all-to-all-start.2 = ((bf16[64,4,4096]{2,1,0:T(4,128)(2,1)}), bf16[64,4,4096]{2,1,0:T(4,128)(2,1)}, u32[]{:S(2)}, u32[]{:S(2)}) async-start(bf16[64,4,4096]{2,1,0:T(4,128)(2,1)} %reshape.104), calls=%async_computation.2 | async-start | bytes 4194304 | tf_op jit(solution)/shard_map/all_to_all | solution.py:139
  297.5 1.7 fusion.36
  299.3 4.0 reshape.98
  303.2 3.0 fusion.3
  306.2 2.1 convolution_convert_fusion.1
  308.3 4.1 reshape.100
  312.4 79.5 %all-to-all-done.2 = bf16[64,4,4096]{2,1,0:T(4,128)(2,1)} async-done(((bf16[64,4,4096]{2,1,0:T(4,128)(2,1)}), bf16[64,4,4096]{2,1,0:T(4,128)(2,1)}, u32[]{:S(2)}, u32[]{:S(2)}) %all-to-all-start.2) | async-done | bytes 2097184 | tf_op jit(solution)/shard_map/all_to_all | solution.py:139
  391.9 6.1 %all-to-all-start.3 = ((bf16[64,4,4096]{2,1,0:T(4,128)(2,1)}), bf16[64,4,4096]{2,1,0:T(4,128)(2,1)}, u32[]{:S(2)}, u32[]{:S(2)}) async-start(bf16[64,4,4096]{2,1,0:T(4,128)(2,1)} %reshape.100), calls=%async_computation.3 | async-start | bytes 4194304 | tf_op jit(solution)/shard_map/all_to_all | solution.py:139
  398.0 1.6 convert.21
  399.6 1.8 fusion.39
  401.5 4.1 reshape.108
  405.6 3.7 convolution_add_fusion.1
  409.3 1.7 reshape.109
  411.1 3.9 multiply_convert_fusion.1
  415.0 0.7 convolution_bitcast_fusion
  415.8 1.7 slice_bitcast_fusion
  417.9 1.3 copy-done.8
  419.2 2.8 collective-permute-start.7
  422.4 1.3 reshape.99
  423.7 1.8 slice.121
  426.3 0.8 copy-done.11
  427.1 1.4 fusion.11
  428.5 65.6 %all-to-all-done.3 = bf16[64,4,4096]{2,1,0:T(4,128)(2,1)} async-done(((bf16[64,4,4096]{2,1,0:T(4,128)(2,1)}), bf16[64,4,4096]{2,1,0:T(4,128)(2,1)}, u32[]{:S(2)}, u32[]{:S(2)}) %all-to-all-start.3) | async-done | bytes 2097184 | tf_op jit(solution)/shard_map/all_to_all | solution.py:139
  494.1 4.0 reshape.105
  498.1 3.3 fusion.4
  501.4 1.7 reshape.106
  503.2 3.3 fusion.21
  506.6 1.3 copy.63
  (80 shorter events, 6.5 us)
Async XLA Ops:
  0.6 176.4 %copy-start = (bf16[128,128]{1,0:T(8,128)(2,1)S(1)}, bf16[128,128]{1,0:T(8,128)(2,1)}, u32[]{:S(2)}) copy-start(bf16[128,128]{1,0:T(8,128)(2,1)} %param.9) | copy-start | bytes 98308
  4.6 2.6 copy-start.3
  7.2 0.7 copy-start.1
  13.0 157.3 %copy-start.4 = (bf16[64,64,128]{2,1,0:T(8,128)(2,1)S(1)}, bf16[64,64,128]{2,1,0:T(8,128)(2,1)}, u32[]{:S(2)}) copy-start(bf16[64,64,128]{2,1,0:T(8,128)(2,1)} %param.8) | copy-start | bytes 3145732
  13.0 175.4 %all-to-all-start = ((bf16[64,4,4096]{2,1,0:T(4,128)(2,1)}), bf16[64,4,4096]{2,1,0:T(4,128)(2,1)}, u32[]{:S(2)}, u32[]{:S(2)}) async-start(bf16[64,4,4096]{2,1,0:T(4,128)(2,1)} %reshape.97), calls=%async_computation | async-start | bytes 4194304 | tf_op jit(solution)/shard_map/all_to_all | solution.py:139
  32.1 144.5 %slice-start = ((bf16[64,64,128]{2,1,0:T(8,128)(2,1)}), bf16[64,56,128]{2,1,0:T(8,128)(2,1)S(1)}, s32[]{:S(2)}) async-start(bf16[64,64,128]{2,1,0:T(8,128)(2,1)} %param.8), calls=%async_computation.4 | async-start | bytes 1835008 | tf_op jit(solution)/shard_map/slice | solution.py:162
  33.9 88.5 %collective-permute-start.1 = (s32[32,4]{0,1:T(4,128)S(1)}, s32[32,4]{0,1:T(4,128)S(1)}, u32[]{:S(2)}, u32[]{:S(2)}) collective-permute-start(s32[32,4]{0,1:T(4,128)S(1)} %bitcast.102), channel_id=1, source_target_pairs={{0,8},{8,16},{16,24},{24,32},{32,40},{40,48},{48,56},{56,64},{64,7... | collective-permute-start | bytes 1544 | tf_op jit(solution)/shard_map/ppermute | solution.py:87
  122.7 9.1 %collective-permute-start.2 = (s32[16,8]{0,1:T(8,128)S(1)}, s32[16,8]{0,1:T(8,128)S(1)}, u32[]{:S(2)}, u32[]{:S(2)}) collective-permute-start(s32[16,8]{0,1:T(8,128)S(1)} %bitcast.98), channel_id=1, source_target_pairs={{0,16},{8,24},{16,32},{24,40},{32,48},{40,56},{48,64},{56,72},{64,... | collective-permute-start | bytes 1544 | tf_op jit(solution)/shard_map/ppermute | solution.py:87
  132.0 6.9 %collective-permute-start.3 = (s32[8,16]{1,0:T(8,128)S(1)}, s32[8,16]{1,0:T(8,128)S(1)}, u32[]{:S(2)}, u32[]{:S(2)}) collective-permute-start(s32[8,16]{1,0:T(8,128)S(1)} %bitcast.100), channel_id=1, source_target_pairs={{0,32},{8,40},{16,48},{24,56},{32,64},{40,72},{48,80},{56,88},{64,... | collective-permute-start | bytes 1544 | tf_op jit(solution)/shard_map/ppermute | solution.py:87
  139.0 7.6 %collective-permute-start.4 = (s32[4,32]{1,0:T(4,128)S(1)}, s32[4,32]{1,0:T(4,128)S(1)}, u32[]{:S(2)}, u32[]{:S(2)}) collective-permute-start(s32[4,32]{1,0:T(4,128)S(1)} %bitcast.104), channel_id=1, source_target_pairs={{0,64},{8,72},{16,80},{24,88},{32,96},{40,104},{48,112},{56,120},{... | collective-permute-start | bytes 1544 | tf_op jit(solution)/shard_map/ppermute | solution.py:87
  146.7 9.8 %collective-permute-start.5 = (s32[2,64]{1,0:T(2,128)S(1)}, s32[2,64]{1,0:T(2,128)S(1)}, u32[]{:S(2)}, u32[]{:S(2)}) collective-permute-start(s32[2,64]{1,0:T(2,128)S(1)} %bitcast.106), channel_id=1, source_target_pairs={{0,128},{8,136},{16,144},{24,152},{32,160},{40,168},{48,176},{56,1... | collective-permute-start | bytes 1544 | tf_op jit(solution)/shard_map/ppermute | solution.py:87
  156.6 15.6 %collective-permute-start.6 = (s32[1,128]{1,0:T(1,128)S(1)}, s32[1,128]{1,0:T(1,128)S(1)}, u32[]{:S(2)}, u32[]{:S(2)}) collective-permute-start(s32[1,128]{1,0:T(1,128)S(1)} %get-tuple-element.29), channel_id=1, source_target_pairs={{0,256},{8,264},{16,272},{24,280},{32,288},{40,296},{48,304},{56,3... | collective-permute-start | bytes 1544 | tf_op jit(solution)/shard_map/ppermute | solution.py:87
  170.4 6.3 %collective-permute-start = (bf16[64,8,128]{2,1,0:T(8,128)(2,1)S(1)}, bf16[64,8,128]{2,1,0:T(8,128)(2,1)S(1)}, u32[]{:S(2)}, u32[]{:S(2)}) collective-permute-start(bf16[64,8,128]{2,1,0:T(8,128)(2,1)S(1)} %slice.77), channel_id=1, source_target_pairs={{0,1},{1,2},{2,3},{3,4},{4,5},{5,6},{6,7},{8,9},{9,10},{10,11},{11... | collective-permute-start | bytes 393224 | tf_op jit(solution)/shard_map/ppermute | solution.py:19
  173.1 3.9 copy-start.14
  178.7 2.1 copy-start.2
  181.6 2.6 copy-start.9
  188.4 103.1 %all-to-all-start.1 = ((bf16[64,4,4096]{2,1,0:T(4,128)(2,1)}), bf16[64,4,4096]{2,1,0:T(4,128)(2,1)}, u32[]{:S(2)}, u32[]{:S(2)}) async-start(bf16[64,4,4096]{2,1,0:T(4,128)(2,1)} %reshape.94), calls=%async_computation.1 | async-start | bytes 4194304 | tf_op jit(solution)/shard_map/all_to_all | solution.py:139
  291.4 100.5 %all-to-all-start.2 = ((bf16[64,4,4096]{2,1,0:T(4,128)(2,1)}), bf16[64,4,4096]{2,1,0:T(4,128)(2,1)}, u32[]{:S(2)}, u32[]{:S(2)}) async-start(bf16[64,4,4096]{2,1,0:T(4,128)(2,1)} %reshape.104), calls=%async_computation.2 | async-start | bytes 4194304 | tf_op jit(solution)/shard_map/all_to_all | solution.py:139
  312.4 85.6 %copy-start.5 = (bf16[64,64,128]{2,1,0:T(8,128)(2,1)S(1)}, bf16[64,64,128]{2,1,0:T(8,128)(2,1)}, u32[]{:S(2)}) copy-start(bf16[64,64,128]{2,1,0:T(8,128)(2,1)} %param.8) | copy-start | bytes 3145732
  391.9 102.1 %all-to-all-start.3 = ((bf16[64,4,4096]{2,1,0:T(4,128)(2,1)}), bf16[64,4,4096]{2,1,0:T(4,128)(2,1)}, u32[]{:S(2)}, u32[]{:S(2)}) async-start(bf16[64,4,4096]{2,1,0:T(4,128)(2,1)} %reshape.100), calls=%async_computation.3 | async-start | bytes 4194304 | tf_op jit(solution)/shard_map/all_to_all | solution.py:139
  401.5 4.1 copy-start.6
  417.8 1.3 copy-start.8
  419.2 7.1 %collective-permute-start.7 = (bf16[64,8,128]{2,1,0:T(8,128)(2,1)S(1)}, bf16[64,8,128]{2,1,0:T(8,128)(2,1)S(1)}, u32[]{:S(2)}, u32[]{:S(2)}) collective-permute-start(bf16[64,8,128]{2,1,0:T(8,128)(2,1)S(1)} %slice.157), channel_id=1, source_target_pairs={{1,0},{2,1},{3,2},{4,3},{5,4},{6,5},{7,6},{9,8},{10,9},{11,10},{12... | collective-permute-start | bytes 393224 | tf_op jit(solution)/shard_map/ppermute | solution.py:19
  423.7 2.1 copy-start.7
  425.9 1.2 copy-start.11
  498.1 5.0 copy-start.13
  501.4 1.7 copy-start.10
  501.4 1.9 copy-start.12

commit v2 on v1

v2 whole, which is shorter than its diff:
```python
import functools

import jax
import jax.numpy as jnp
from jax import lax
from jax.experimental import pallas as pl
from jax.experimental.pallas import tpu as pltpu
from jax.sharding import PartitionSpec as P

DILATION = 8
CAPACITY = 4
LANES = 128
SHARE = 16

ROWS_BY_ROWS = (((1,), (1,)), ((), ()))
COLUMNS_BY_COLUMNS = (((0,), (0,)), ((), ()))
VMEM = pl.BlockSpec(memory_space=pltpu.VMEM)


def from_behind(value, axis, by):
    count = lax.axis_size(axis)
    pairs = [(i, i + by) for i in range(count) if 0 <= i + by < count]
    return lax.ppermute(value, axis, pairs)


def mm(left, right):
    return jnp.dot(left, right, preferred_element_type=jnp.float32)


def mm_t(left, right):
    return lax.dot_general(left, right, ROWS_BY_ROWS, preferred_element_type=jnp.float32)


def t_mm(left, right):
    return lax.dot_general(left, right, COLUMNS_BY_COLUMNS, preferred_element_type=jnp.float32)


def graph_kernel(peers, me_ref, index_ref, count_ref, weight_ref, graph_ref, member_all, owner_all):
    sensors, slots = index_ref.shape
    places = peers * CAPACITY
    half = (places + sensors) // 2
    me = me_ref[0]
    index = index_ref[...].T
    live = lax.broadcasted_iota(jnp.int32, (slots, sensors), 0) < count_ref[...]
    masked = jnp.where(live, weight_ref[...].T, 0.0)
    trans = masked / jnp.sum(masked, axis=0, keepdims=True)
    owner = jnp.where(live, index // sensors, -1)
    member = index % sensors
    member_ids = lax.broadcasted_iota(jnp.int32, (sensors, sensors), 0)
    owner_ids = lax.broadcasted_iota(jnp.int32, (peers, sensors), 0)
    for j in range(slots):
        place = slice(j * sensors, (j + 1) * sensors)
        hit = member_ids == member[j : j + 1]
        member_all[:, place] = jnp.where(hit, 1.0, 0.0).astype(jnp.bfloat16)
        owner_all[:, place] = jnp.where(owner_ids == owner[j : j + 1], 1.0, 0.0).astype(jnp.bfloat16)
    named = mm_t(owner_all[...], member_all[...])
    named = (named > 0.0) & (owner_ids != me)
    flags = jnp.where(named, 1.0, 0.0).astype(jnp.bfloat16)
    below = lax.broadcasted_iota(jnp.int32, (sensors, sensors), 0) < lax.broadcasted_iota(
        jnp.int32, (sensors, sensors), 1
    )
    rank = mm(flags, jnp.where(below, 1.0, 0.0).astype(jnp.bfloat16))
    spread_rank = jnp.where(named, rank, 255.0).astype(jnp.bfloat16)
    ranks = mm(rank.astype(jnp.bfloat16), member_all[...])
    ranks = jnp.where(owner_all[...] > 0, ranks, 0.0)
    ranks = jnp.sum(ranks, axis=0, keepdims=True)
    ranks = jnp.concatenate([ranks[:, j * sensors : (j + 1) * sensors] for j in range(slots)], axis=0)
    distant = owner * CAPACITY + ranks.astype(jnp.int32)
    row = jnp.where(owner == me, places + member, distant) - half
    row = jnp.where(live, row, half)
    graph_ref[...] = jnp.zeros(graph_ref.shape, jnp.bfloat16)
    graph_ref[0:slots, :] = row.astype(jnp.float32).astype(jnp.bfloat16)
    graph_ref[slots : 2 * slots, :] = trans.astype(jnp.bfloat16)
    expand = lax.broadcasted_iota(jnp.int32, (places, peers), 0) // CAPACITY == lax.broadcasted_iota(
        jnp.int32, (places, peers), 1
    )
    spread_rank = mm(jnp.where(expand, 1.0, 0.0).astype(jnp.bfloat16), spread_rank)
    wanted_rank = (lax.broadcasted_iota(jnp.int32, (places, sensors), 0) % CAPACITY).astype(jnp.float32)
    chosen = jnp.where(spread_rank == wanted_rank, 1.0, 0.0).astype(jnp.bfloat16)
    lane_ids = lax.broadcasted_iota(jnp.int32, (SHARE, sensors), 1).astype(jnp.float32)
    first_row = lax.broadcasted_iota(jnp.int32, (SHARE, sensors), 0) == 0
    label = jnp.where(first_row, lane_ids, 1.0).astype(jnp.bfloat16)
    asked = mm_t(label, chosen)
    asked = jnp.where(asked[1:2] > 0.5, asked[0:1], -1.0)
    asked = jnp.concatenate([asked[:, i * sensors : (i + 1) * sensors] for i in range(places // sensors)], axis=0)
    asked = jnp.concatenate([asked, jnp.zeros((SHARE - asked.shape[0], sensors), jnp.float32)], axis=0)
    graph_ref[2 * slots : 2 * slots + SHARE, :] = asked.astype(jnp.bfloat16)


def own_graph(peers, shares, myself, index, count, weight):
    sensors, slots = index.shape
    return pl.pallas_call(
        functools.partial(graph_kernel, peers),
        out_shape=jax.ShapeDtypeStruct((shares * SHARE, sensors), jnp.bfloat16),
        in_specs=[pl.BlockSpec(memory_space=pltpu.SMEM), VMEM, VMEM, VMEM],
        out_specs=VMEM,
        scratch_shapes=[
            pltpu.VMEM((sensors, slots * sensors), jnp.bfloat16),
            pltpu.VMEM((peers, slots * sensors), jnp.bfloat16),
        ],
        compiler_params=pltpu.CompilerParams(vmem_limit_bytes=32 * 1024 * 1024),
        cost_estimate=pl.CostEstimate(flops=4 * 10**8, bytes_accessed=10**6, transcendentals=0),
        name="own_graph",
    )(myself.reshape(1).astype(jnp.int32), index, count.reshape(1, sensors), weight)


def tables_kernel(slots, group, graph_ref, asked_ref, table_ref, pick_ref):
    rows, sensors = table_ref.shape[1:]
    places = rows - sensors
    chunk = 64
    for i in range(group):
        per_share = graph_ref.shape[2]
        codes = [graph_ref[j // per_share, i, j % per_share : j % per_share + 1, :].astype(jnp.float32) for j in range(slots)]
        weights = [
            graph_ref[(slots + j) // per_share, i, j % per_share : j % per_share + 1, :].astype(jnp.float32)
            for j in range(slots)
        ]
        for start in range(0, rows, chunk):
            ids = lax.broadcasted_iota(jnp.int32, (chunk, sensors), 0).astype(jnp.float32) + (start - rows // 2)
            total = jnp.zeros((chunk, sensors), jnp.float32)
            for j in range(slots):
                total = jnp.where(ids == codes[j], weights[j], total)
            table_ref[i, start : start + chunk, :] = total.astype(jnp.bfloat16)
        own_ids = lax.broadcasted_iota(jnp.int32, (sensors, places), 0).astype(jnp.float32)
        asked = asked_ref[i : i + 1, :]
        pick_ref[i] = jnp.where(own_ids == asked, 1.0, 0.0).astype(jnp.bfloat16)


def all_tables(slots, graph, asked):
    shares, peers, per_share, sensors = graph.shape
    places = asked.shape[1]
    group = 8
    return pl.pallas_call(
        functools.partial(tables_kernel, slots, group),
        grid=(peers // group,),
        out_shape=(
            jax.ShapeDtypeStruct((peers, places + sensors, sensors), jnp.bfloat16),
            jax.ShapeDtypeStruct((peers, sensors, places), jnp.bfloat16),
        ),
        in_specs=[
            pl.BlockSpec((shares, group, per_share, sensors), lambda i: (0, i, 0, 0)),
            pl.BlockSpec((group, places), lambda i: (i, 0)),
        ],
        out_specs=(
            pl.BlockSpec((group, places + sensors, sensors), lambda i: (i, 0, 0)),
            pl.BlockSpec((group, sensors, places), lambda i: (i, 0, 0)),
        ),
        compiler_params=pltpu.CompilerParams(vmem_limit_bytes=32 * 1024 * 1024),
        cost_estimate=pl.CostEstimate(flops=2 * 10**8, bytes_accessed=12 * 10**6, transcendentals=0),
        name="all_tables",
    )(graph, asked)


def swap_places(gathered, pair, left, right):
    count = left.shape[0]
    low = lax.broadcasted_iota(jnp.int32, left.shape, 0) % (2 * CAPACITY) < CAPACITY
    even = jnp.where(low, left, pltpu.roll(right, CAPACITY, 0))
    odd = jnp.where(low, pltpu.roll(left, count - CAPACITY, 0), right)
    at = pl.ds(pl.multiple_of(pair * 2 * CAPACITY, 2 * CAPACITY), 2 * CAPACITY)
    shape = (count // (2 * CAPACITY), 2 * CAPACITY, left.shape[1])
    gathered[:, 0, at, :] = even.reshape(shape)
    gathered[:, 1, at, :] = odd.reshape(shape)


def back_kernel(places, grad_ref, weight_ref, table_ref, pick_ref, out_ref, base, second, first, gathered):
    peers, channels, sensors = grad_ref.shape

    @pl.loop(0, peers)
    def _(p):
        theta = t_mm(grad_ref[p], weight_ref[...])
        base[p] = theta[:, :LANES]
        second[p] = theta[:, LANES:].astype(jnp.bfloat16)

    def hop(source, finish):
        @pl.loop(0, peers // 2)
        def _(pair):
            left = mm(table_ref[2 * pair, :places, :], source[2 * pair])
            right = mm(table_ref[2 * pair + 1, :places, :], source[2 * pair + 1])
            swap_places(gathered, pair, left, right)

        @pl.loop(0, peers // 2)
        def _(pair):
            for side in range(2):
                p = 2 * pair + side
                far = mm(pick_ref[p], gathered[pair, side].astype(jnp.bfloat16))
                finish(p, far + mm(table_ref[p, places:, :], source[p]))

    def keep_first(p, value):
        first[p] = (base[p] + value).astype(jnp.bfloat16)

    def keep_out(p, value):
        out_ref[p] = value.T[:channels].astype(jnp.bfloat16)

    hop(second, keep_first)
    hop(first, keep_out)


def forward_kernel(places, hidden_ref, unit_ref, one_ref, two_ref, table_ref, pick_ref, out_ref, start, middle, gathered):
    peers, channels, sensors = hidden_ref.shape

    @pl.loop(0, peers)
    def _(p):
        start[p] = t_mm(hidden_ref[p], unit_ref[...]).astype(jnp.bfloat16)

    def hop(source, finish):
        @pl.loop(0, peers // 2)
        def _(pair):
            left = t_mm(pick_ref[2 * pair], source[2 * pair])
            right = t_mm(pick_ref[2 * pair + 1], source[2 * pair + 1])
            swap_places(gathered, pair, left, right)

        @pl.loop(0, peers // 2)
        def _(pair):
            for side in range(2):
                p = 2 * pair + side
                far = t_mm(table_ref[p, :places, :], gathered[pair, side].astype(jnp.bfloat16))
                finish(p, (far + t_mm(table_ref[p, places:, :], source[p])).astype(jnp.bfloat16))

    def keep_middle(p, value):
        middle[p] = value

    def keep_out(p, value):
        mixed = mm_t(one_ref[...], middle[p]) + mm_t(two_ref[...], value)
        out_ref[p] = mixed.astype(jnp.bfloat16)

    hop(start, keep_middle)
    hop(middle, keep_out)


def to_lanes(block):
    return jnp.pad(block, ((0, 0), (0, LANES - block.shape[1])))


def back_hops(grad, diff_weight, table, pick):
    peers, channels, sensors = grad.shape
    places = pick.shape[2]
    weight = jnp.concatenate(
        [to_lanes(diff_weight[:, channels : 2 * channels]), to_lanes(diff_weight[:, 2 * channels :])], axis=1
    )
    return pl.pallas_call(
        functools.partial(back_kernel, places),
        out_shape=jax.ShapeDtypeStruct(grad.shape, jnp.bfloat16),
        in_specs=[VMEM] * 4,
        out_specs=VMEM,
        scratch_shapes=[
            pltpu.VMEM((peers, sensors, LANES), jnp.float32),
            pltpu.VMEM((peers, sensors, LANES), jnp.bfloat16),
            pltpu.VMEM((peers, sensors, LANES), jnp.bfloat16),
            pltpu.VMEM((peers // 2, 2, peers * CAPACITY, LANES), jnp.float32),
        ],
        compiler_params=pltpu.CompilerParams(vmem_limit_bytes=48 * 1024 * 1024),
        cost_estimate=pl.CostEstimate(flops=3 * 10**9, bytes_accessed=12 * 10**6, transcendentals=0),
        name="back_hops",
    )(grad, weight, table, pick)


def forward_hops(hidden, diff_weight, table, pick):
    peers, channels, sensors = hidden.shape
    places = pick.shape[2]
    unit = to_lanes(jnp.eye(channels, dtype=jnp.bfloat16))
    one = to_lanes(diff_weight[:, channels : 2 * channels])
    two = to_lanes(diff_weight[:, 2 * channels :])
    return pl.pallas_call(
        functools.partial(forward_kernel, places),
        out_shape=jax.ShapeDtypeStruct(hidden.shape, jnp.bfloat16),
        in_specs=[VMEM] * 6,
        out_specs=VMEM,
        scratch_shapes=[
            pltpu.VMEM((peers, sensors, LANES), jnp.bfloat16),
            pltpu.VMEM((peers, sensors, LANES), jnp.bfloat16),
            pltpu.VMEM((peers // 2, 2, peers * CAPACITY, LANES), jnp.float32),
        ],
        compiler_params=pltpu.CompilerParams(vmem_limit_bytes=48 * 1024 * 1024),
        cost_estimate=pl.CostEstimate(flops=3 * 10**9, bytes_accessed=12 * 10**6, transcendentals=0),
        name="forward_hops",
    )(hidden, unit, one, two, table, pick)


def exchange(blocks, earlier=None):
    if earlier is not None:
        blocks, earlier = lax.optimization_barrier((blocks, earlier))
    return lax.all_to_all(blocks, "sensor", split_axis=0, concat_axis=0, tiled=True)


def asked_of(graph, slots, peer_count):
    sensors = graph.shape[3]
    rows = graph[2 * slots // SHARE, :, : peer_count * CAPACITY // sensors, :]
    rows = rows.reshape(peer_count, peer_count, CAPACITY).transpose(1, 0, 2)
    return rows.reshape(peer_count, peer_count * CAPACITY).astype(jnp.float32)


def per_device(
    signal,
    conv_weight,
    conv_bias,
    diff_weight,
    neighbour_index,
    neighbour_count,
    edge_weight,
    cotangent,
):
    channels, step_count, sensor_count = signal.shape
    slots = neighbour_index.shape[1]
    peer_count = lax.axis_size("sensor")
    share_count = lax.axis_size("tm")

    graph = own_graph(
        peer_count, share_count, lax.axis_index("sensor"), neighbour_index, neighbour_count, edge_weight
    )
    share = lax.dynamic_slice_in_dim(graph, lax.axis_index("tm") * SHARE, SHARE, 0)
    share = exchange(jnp.broadcast_to(share[None], (peer_count, SHARE, sensor_count)))
    grad_in = exchange(cotangent.transpose(1, 0, 2), share)
    graphs = lax.all_gather(share, "tm", axis=0, tiled=False)
    table, pick = all_tables(slots, graphs, asked_of(graphs, slots, peer_count))

    tail_steps = signal[:, step_count - DILATION :, :]
    before = from_behind(tail_steps, "tm", 1)
    lagged = jnp.concatenate([before, signal[:, : step_count - DILATION, :]], axis=1)
    stacked = jnp.concatenate([lagged, signal], axis=0).reshape(
        2 * channels, step_count * sensor_count
    )
    preact = mm(conv_weight, stacked) + conv_bias[:, None]
    tanh_part = jnp.tanh(preact[:channels])
    gate_part = jax.nn.sigmoid(preact[channels:])
    hidden = (tanh_part * gate_part).astype(jnp.bfloat16)
    hidden_in = exchange(
        hidden.reshape(channels, step_count, sensor_count).transpose(1, 0, 2), grad_in
    )

    grad_out = exchange(back_hops(grad_in, diff_weight, table, pick), hidden_in)
    mixed_out = exchange(forward_hops(hidden_in, diff_weight, table, pick), grad_out)

    theta_back = lax.dot_general(
        diff_weight[:, :channels],
        cotangent.reshape(channels, -1),
        COLUMNS_BY_COLUMNS,
        preferred_element_type=jnp.float32,
    )
    grad_hidden = theta_back + grad_out.transpose(1, 0, 2).reshape(channels, -1).astype(jnp.float32)
    grad_tanh = grad_hidden * gate_part * (1.0 - tanh_part * tanh_part)
    grad_gate = grad_hidden * tanh_part * gate_part * (1.0 - gate_part)
    grad_pre = jnp.concatenate([grad_tanh, grad_gate], axis=0).astype(jnp.bfloat16)
    conv_back = lax.dot_general(
        conv_weight, grad_pre, COLUMNS_BY_COLUMNS, preferred_element_type=jnp.float32
    )
    lag_back = conv_back[:channels].reshape(channels, step_count, sensor_count)
    now_back = conv_back[channels:].reshape(channels, step_count, sensor_count)
    after = from_behind(lag_back[:, :DILATION, :].astype(jnp.bfloat16), "tm", -1).astype(
        jnp.float32
    )
    shifted = jnp.concatenate([lag_back[:, DILATION:, :], after], axis=1)
    grad_signal = (cotangent.astype(jnp.float32) + now_back + shifted).astype(jnp.bfloat16)

    kept = signal.astype(jnp.float32) + mm(diff_weight[:, :channels], hidden).reshape(signal.shape)
    output = (kept + mixed_out.transpose(1, 0, 2).astype(jnp.float32)).astype(jnp.bfloat16)
    return (output, grad_signal)


def solution(mesh):
    placed = (
        P(None, "tm", "sensor"),
        P(),
        P(),
        P(),
        P("sensor", None),
        P("sensor"),
        P("sensor", None),
        P(None, "tm", "sensor"),
    )
    return jax.shard_map(
        per_device,
        mesh=mesh,
        in_specs=placed,
        out_specs=(P(None, "tm", "sensor"), P(None, "tm", "sensor")),
        check_vma=False,
    )
```

time: 515 us -> 358 us (0.70); the launches traced: 508 us -> 357 us
  waiting for transfers between devices: 324 us -> 105 us
  Pallas kernels: 2.16 us -> 137 us
  local copies, waits for them, and re-layouts: 56.6 us -> 16.9 us
  matrix products: 35.1 us -> 11.3 us
  between operations: 1.11 us -> 14.4 us
  starting transfers between devices: 77.4 us -> 64.2 us
    pallas_call x1 -> x4, Pallas kernels: 2.16 us -> 137 us  [the longest x1 53.1 us: forward_hops(): pl.pallas_call(functools.partial(forward_kernel, places), out_shape=jax.S...]
    all_to_all x4 -> x5, waiting for transfers between devices: 216 us -> 100 us  [exchange(): lax.all_to_all(blocks, 'sensor', split_axis=0, concat_axis=0, tiled=True)]
    ppermute x6 -> x0, waiting for transfers between devices: 104 us -> none  [swap_requests(): lax.ppermute(parts[:, 1], axis, [(i, (i + step) % count) for i in range(c...]
    reshape x18 -> x0, local copies, waits for them, and re-layouts: 39.9 us -> none  [the longest x4 16 us: absorb(): arrived.reshape(peer_count * CAPACITY, row_count)]
    ppermute x6 -> x0, starting transfers between devices: 31.5 us -> none  [swap_requests(): lax.ppermute(parts[:, 1], axis, [(i, (i + step) % count) for i in range(c...]
    dot_general x12 -> x2, matrix products: 27.9 us -> 4.98 us  [the longest x1 4.23 us: per_device(): lax.dot_general(diff_weight[:, :channels], cotangent.reshape(channels, -1...]
    all_to_all x4 -> x5, starting transfers between devices: 41.1 us -> 59.8 us  [exchange(): lax.all_to_all(blocks, 'sensor', split_axis=0, concat_axis=0, tiled=True)]
    unnamed x36 -> x33, local copies, waits for them, and re-layouts: 12.7 us -> 14 us
  transfers between devices with their start and end apart: 12 -> 8, of which waited for: 9 -> 4; matrix products, arithmetic and copies ran while one was open for 15% -> 6% of each run, Pallas kernels for 0% -> 38%
where the time goes in v2:
time: 358 us; the launch traced here: 357 us
  Pallas kernels  137 us (38%)
  waiting for transfers between devices  105 us (29%)
  starting transfers between devices  64.2 us (18%)
  local copies, waits for them, and re-layouts  16.9 us (5%)
  between operations  14.4 us (4%)
  matrix products  11.3 us (3%)
  other arithmetic  9.09 us (3%)
    all_to_all x5, waiting for transfers between devices, exchange(): lax.all_to_all(blocks, 'sensor', split_axis=0, concat_axis=0, tiled=True)  100 us
    all_to_all x5, starting transfers between devices, exchange(): lax.all_to_all(blocks, 'sensor', split_axis=0, concat_axis=0, tiled=True)  59.8 us
    pallas_call x1, Pallas kernels, forward_hops(): pl.pallas_call(functools.partial(forward_kernel, places), out_shape=jax.S...  53.1 us
    pallas_call x1, Pallas kernels, back_hops(): pl.pallas_call(functools.partial(back_kernel, places), out_shape=jax.Shap...  44.3 us
    pallas_call x1, Pallas kernels, all_tables(): pl.pallas_call(functools.partial(tables_kernel, slots, group), grid=(peer...  37.8 us
    unnamed x33, local copies, waits for them, and re-layouts  14 us
  transfers between devices with their start and end apart: 8, of which 4 were waited for; matrix products, arithmetic and copies ran while one was open for 6% of the time, Pallas kernels for 38%

profile of v2, /device:TPU:6, one launch (start us, length us, event | category | flops | bytes accessed | tf_op | source)
XLA Modules:
  0.0 357.2 jit_solution(4329109700181185315)
XLA Ops:
  7.2 0.0 copy-start
  7.2 0.8 copy.42.index_ref
  8.0 0.8 copy.43.weight_ref
  8.8 0.0 copy-start.4
  8.8 0.6 copy-done.4
  9.5 1.5 own_graph.1
  11.0 0.7 broadcast_in_dim.2
  11.8 18.7 %all-to-all-start = ((bf16[64,16,128]{2,1,0:T(8,128)(2,1)}), bf16[64,16,128]{2,1,0:T(8,128)(2,1)S(1)}, u32[]{:S(2)}, u32[]{:S(2)}) async-start(bf16[64,16,128]{2,1,0:T(8,128)(2,1)} %broadcast_in_dim.2), calls=%async_computation | async-start | bytes 524288 | tf_op jit(solution)/shard_map/all_to_all | solution.py:282
  30.5 0.0 copy-done.7
  30.5 0.0 copy-start.6
  30.5 1.6 copy.71
  32.2 20.8 %all-to-all-done = bf16[64,16,128]{2,1,0:T(8,128)(2,1)S(1)} async-done(((bf16[64,16,128]{2,1,0:T(8,128)(2,1)}), bf16[64,16,128]{2,1,0:T(8,128)(2,1)S(1)}, u32[]{:S(2)}, u32[]{:S(2)}) %all-to-all-start) | async-done | bytes 262176 | tf_op jit(solution)/shard_map/all_to_all | solution.py:282
  53.0 5.1 %all-to-all-start.1 = ((bf16[64,64,128]{2,1,0:T(8,128)(2,1)}), bf16[64,64,128]{2,1,0:T(8,128)(2,1)S(1)}, u32[]{:S(2)}, u32[]{:S(2)}) async-start(bf16[64,64,128]{2,1,0:T(8,128)(2,1)} %bitcast.68), calls=%async_computation.1 | async-start | bytes 2097152 | tf_op jit(solution)/shard_map/all_to_all | solution.py:282
  58.1 0.0 all-gather.3.cloned.1.call-start
  58.1 0.0 copy-done.6
  58.2 1.9 collective-permute-start
  60.1 0.0 copy-done.10
  60.1 0.0 copy-start.12
  60.1 4.3 %collective-permute-done = bf16[64,8,128]{2,1,0:T(8,128)(2,1)S(1)} collective-permute-done((bf16[64,8,128]{2,1,0:T(8,128)(2,1)S(1)}, bf16[64,8,128]{2,1,0:T(8,128)(2,1)S(1)}, u32[]{:S(2)}, u32[]{:S(2)}) %collective-permute-start) | collective-permute-done | bytes 131104 | tf_op jit(solution)/shard_map/ppermute | solution.py:23
  64.5 0.0 slice-done
  64.5 0.3 pad_maximum_fusion
  64.8 0.0 copy-done
  64.8 0.0 copy-done.12
  64.8 3.8 %fusion = f32[128,8192]{1,0:T(8,128)} fusion(bf16[128,128]{1,0:T(8,128)(2,1)S(1)} %copy-done, bf16[16,8,64,128]{3,2,1,0:T(8,128)(2,1)S(1)} %bitcast.65, f32[128]{0:T(128)S(1)} %copy-done.12), kind=kOutput, calls=%fused_computation.1 | convolution fusion | flops 269484032 | bytes 6324736 | tf_op jit(solution)/shard_map/dot_general | solution.py:27
  68.5 0.0 all-gather.3.cloned.1.call-update
  68.6 4.0 %bitcast_bitcast_fusion = bf16[64,64,128]{2,1,0:T(8,128)(2,1)} fusion(f32[128,8192]{1,0:T(8,128)} %fusion), kind=kLoop, calls=%fused_computation.30 | loop fusion | flops 2621440 | bytes 5242880 | tf_op jit(solution)/shard_map/transpose | solution.py:327
  72.6 39.9 %all-to-all-done.1.grad_ref = bf16[64,64,128]{2,1,0:T(8,128)(2,1)S(1)} async-done(((bf16[64,64,128]{2,1,0:T(8,128)(2,1)}), bf16[64,64,128]{2,1,0:T(8,128)(2,1)S(1)}, u32[]{:S(2)}, u32[]{:S(2)}) %all-to-all-start.1) | async-done | bytes 1048608 | tf_op jit(solution)/shard_map/all_to_all | solution.py:282
  112.5 6.0 %all-to-all-start.2 = ((bf16[64,64,128]{2,1,0:T(8,128)(2,1)}), bf16[64,64,128]{2,1,0:T(8,128)(2,1)S(1)}, u32[]{:S(2)}, u32[]{:S(2)}) async-start(bf16[64,64,128]{2,1,0:T(8,128)(2,1)} %bitcast_bitcast_fusion), calls=%async_computation.2 | async-start | bytes 2097152 | tf_op jit(solution)/shard_map/all_to_all | solution.py:282
  118.5 0.0 copy-done.11
  118.5 0.1 fusion.18
  118.7 0.0 all-gather.3.cloned.1.call-done
  118.7 0.9 slice_convert_fusion.1
  119.6 0.1 copy.44
  119.7 0.8 copy.45
  120.5 1.0 copy.46.asked_ref
  121.5 0.0 copy-start.3
  121.5 1.6 copy-done.3
  123.1 37.8 %all_tables.1 = (bf16[64,384,128]{2,1,0:T(8,128)(2,1)S(1)}, bf16[64,128,256]{2,1,0:T(8,128)(2,1)S(1)}) custom-call(bf16[8,64,16,128]{3,2,1,0:T(8,128)(2,1)S(1)} %bitcast.63, f32[64,256]{1,0:T(8,128)S(1)} %copy.46.asked_ref), custom_call_target="tpu_custom_call" | custom-call | flops 200000000 | bytes 12000000 | tf_op jit(solution)/shard_map/all_tables/pallas_call | solution.py:133
  160.9 0.0 copy-start.1
  160.9 2.6 copy-done.1
  163.5 2.0 copy-done.2
  165.5 44.3 %back_hops.1 = bf16[64,64,128]{2,1,0:T(8,128)(2,1)} custom-call(bf16[64,64,128]{2,1,0:T(8,128)(2,1)S(1)} %all-to-all-done.1.grad_ref, bf16[64,256]{1,0:T(8,128)(2,1)S(1)} %pad_maximum_fusion.1.weight_ref, bf16[64,384,128]{2,1,0:T(8,128)(2,1)} %copy-done.1, bf16[64,128,256]{2,1,0:T(8,128)(2,1)} %copy-done.2), custom_call_target="tpu_custom_call" | custom-call | flops 3000000000 | bytes 12000000 | tf_op jit(solution)/shard_map/back_hops/pallas_call | solution.py:240
  209.8 0.0 all-to-all-done.2.hidden_ref
  209.8 14.9 %all-to-all-start.3 = ((bf16[64,64,128]{2,1,0:T(8,128)(2,1)}), bf16[64,64,128]{2,1,0:T(8,128)(2,1)S(1)}, u32[]{:S(2)}, u32[]{:S(2)}) async-start(bf16[64,64,128]{2,1,0:T(8,128)(2,1)} %back_hops.1), calls=%async_computation.3 | async-start | bytes 2097152 | tf_op jit(solution)/shard_map/all_to_all | solution.py:282
  224.7 53.1 %forward_hops.1 = bf16[64,64,128]{2,1,0:T(8,128)(2,1)} custom-call(bf16[64,64,128]{2,1,0:T(8,128)(2,1)S(1)} %all-to-all-done.2.hidden_ref, bf16[64,128]{1,0:T(8,128)(2,1)S(1)} %pad_convert_fusion.unit_ref, bf16[64,128]{1,0:T(8,128)(2,1)S(1)} %pad.16.one_ref, bf16[64,128]{1,0:T(8,128)(2,1)S(1)} %pad.17.two_ref, bf16[64,384,128]{2,1,0:T(8,128)(2,1)} %copy-done.1, ...), custom_call_target="tpu_custom_call" | custom-call | flops 3000000000 | bytes 12000000 | tf_op jit(solution)/shard_map/forward_hops/pallas_call | solution.py:263
  277.8 0.0 all-to-all-done.3
  277.8 1.0 copy-done.9
  278.8 15.1 %all-to-all-start.4 = ((bf16[64,64,128]{2,1,0:T(8,128)(2,1)}), bf16[64,64,128]{2,1,0:T(8,128)(2,1)S(1)}, u32[]{:S(2)}, u32[]{:S(2)}) async-start(bf16[64,64,128]{2,1,0:T(8,128)(2,1)} %forward_hops.1), calls=%async_computation.4 | async-start | bytes 2097152 | tf_op jit(solution)/shard_map/all_to_all | solution.py:282
  293.9 0.0 copy-done.8
  293.9 4.2 %multiply_convert_fusion.1 = (bf16[64,8192]{1,0:T(8,128)(2,1)S(1)}, bf16[64,8192]{1,0:T(8,128)(2,1)S(1)}) fusion(f32[128,8192]{1,0:T(8,128)} %fusion, bf16[8,8,64,128]{3,2,1,0:T(8,128)(2,1)S(1)} %bitcast.69, bf16[64,192]{1,0:T(8,128)(2,1)S(1)} %copy-done.11, bf16[64,64,128]{2,1,0:T(8,128)(2,1)} %copy-done.9), kind=kOutput, calls=%fused_computation.25 | convolution fusion | flops 74973184 | bytes 8404992 | tf_op jit(solution)/shard_map/dot_general | solution.py:333
  298.2 0.7 convolution_bitcast_fusion
  298.9 0.4 slice_bitcast_fusion
  299.3 0.0 copy-start.5
  299.3 0.4 copy.55
  299.7 2.4 collective-permute-start.1
  302.1 0.0 copy-done.5
  302.2 2.5 convolution_bitcast_fusion.1
  304.7 0.2 slice.57
  304.8 0.4 copy.54
  305.2 0.0 collective-permute-done.1
  305.2 1.4 fusion.2
  306.7 39.7 %all-to-all-done.4 = bf16[64,64,128]{2,1,0:T(8,128)(2,1)S(1)} async-done(((bf16[64,64,128]{2,1,0:T(8,128)(2,1)}), bf16[64,64,128]{2,1,0:T(8,128)(2,1)S(1)}, u32[]{:S(2)}, u32[]{:S(2)}) %all-to-all-start.4) | async-done | bytes 1048608 | tf_op jit(solution)/shard_map/all_to_all | solution.py:282
  346.4 2.4 fusion.6
  348.7 1.6 copy.48
  (16 shorter events, 0.2 us)
Async XLA Ops:
  7.2 57.6 %copy-start = (bf16[128,128]{1,0:T(8,128)(2,1)S(1)}, bf16[128,128]{1,0:T(8,128)(2,1)}, u32[]{:S(2)}) copy-start(bf16[128,128]{1,0:T(8,128)(2,1)} %param.9) | copy-start | bytes 98308
  8.8 0.7 copy-start.4
  9.5 21.0 %copy-start.7 = (bf16[64,64,128]{2,1,0:T(8,128)(2,1)S(1)}, bf16[64,64,128]{2,1,0:T(8,128)(2,1)}, u32[]{:S(2)}) copy-start(bf16[64,64,128]{2,1,0:T(8,128)(2,1)} %param.15) | copy-start | bytes 3145732
  11.8 41.2 %all-to-all-start = ((bf16[64,16,128]{2,1,0:T(8,128)(2,1)}), bf16[64,16,128]{2,1,0:T(8,128)(2,1)S(1)}, u32[]{:S(2)}, u32[]{:S(2)}) async-start(bf16[64,16,128]{2,1,0:T(8,128)(2,1)} %broadcast_in_dim.2), calls=%async_computation | async-start | bytes 524288 | tf_op jit(solution)/shard_map/all_to_all | solution.py:282
  30.5 27.6 %copy-start.6 = (bf16[64,64,128]{2,1,0:T(8,128)(2,1)S(1)}, bf16[64,64,128]{2,1,0:T(8,128)(2,1)}, u32[]{:S(2)}) copy-start(bf16[64,64,128]{2,1,0:T(8,128)(2,1)} %param.8) | copy-start | bytes 3145732
  53.0 7.1 %copy-start.10 = (bf16[64,16,128]{2,1,0:T(8,128)(2,1)}, bf16[64,16,128]{2,1,0:T(8,128)(2,1)S(1)}, u32[]{:S(2)}) copy-start(bf16[64,16,128]{2,1,0:T(8,128)(2,1)S(1)} %all-to-all-done) | copy-start | bytes 786436
  53.0 11.5 %slice-start = ((bf16[64,64,128]{2,1,0:T(8,128)(2,1)}), bf16[64,56,128]{2,1,0:T(8,128)(2,1)S(1)}, s32[]{:S(2)}) async-start(bf16[64,64,128]{2,1,0:T(8,128)(2,1)} %param.8), calls=%async_computation.6 | async-start | bytes 1835008 | tf_op jit(solution)/shard_map/slice | solution.py:318
  53.0 59.5 %all-to-all-start.1 = ((bf16[64,64,128]{2,1,0:T(8,128)(2,1)}), bf16[64,64,128]{2,1,0:T(8,128)(2,1)S(1)}, u32[]{:S(2)}, u32[]{:S(2)}) async-start(bf16[64,64,128]{2,1,0:T(8,128)(2,1)} %bitcast.68), calls=%async_computation.1 | async-start | bytes 2097152 | tf_op jit(solution)/shard_map/all_to_all | solution.py:282
  58.1 60.6 %all-gather.3.cloned.1.call-start = ((), (), s32[]{:S(2)}) async-start(), calls=%async_computation.5 | async-start | bytes 2359296 | tf_op jit(solution)/shard_map/all_gather | solution.py:313
  58.2 6.3 %collective-permute-start = (bf16[64,8,128]{2,1,0:T(8,128)(2,1)S(1)}, bf16[64,8,128]{2,1,0:T(8,128)(2,1)S(1)}, u32[]{:S(2)}, u32[]{:S(2)}) collective-permute-start(bf16[64,8,128]{2,1,0:T(8,128)(2,1)S(1)} %slice.40), channel_id=1, source_target_pairs={{0,1},{1,2},{2,3},{3,4},{4,5},{5,6},{6,7},{8,9},{9,10},{10,11},{11... | collective-permute-start | bytes 393224 | tf_op jit(solution)/shard_map/ppermute | solution.py:23
  60.1 4.7 %copy-start.12 = (f32[128]{0:T(128)S(1)}, f32[128]{0:T(128)}, u32[]{:S(2)}) copy-start(f32[128]{0:T(128)} %param.10) | copy-start | bytes 1540
  72.6 46.0 %copy-start.11 = (bf16[64,192]{1,0:T(8,128)(2,1)S(1)}, bf16[64,192]{1,0:T(8,128)(2,1)}, u32[]{:S(2)}) copy-start(bf16[64,192]{1,0:T(8,128)(2,1)} %param.11) | copy-start | bytes 73732
  112.5 97.3 %all-to-all-start.2 = ((bf16[64,64,128]{2,1,0:T(8,128)(2,1)}), bf16[64,64,128]{2,1,0:T(8,128)(2,1)S(1)}, u32[]{:S(2)}, u32[]{:S(2)}) async-start(bf16[64,64,128]{2,1,0:T(8,128)(2,1)} %bitcast_bitcast_fusion), calls=%async_computation.2 | async-start | bytes 2097152 | tf_op jit(solution)/shard_map/all_to_all | solution.py:282
  121.5 1.6 copy-start.3
  160.9 2.6 copy-start.1
  163.5 2.0 copy-start.2
  209.8 68.0 %all-to-all-start.3 = ((bf16[64,64,128]{2,1,0:T(8,128)(2,1)}), bf16[64,64,128]{2,1,0:T(8,128)(2,1)S(1)}, u32[]{:S(2)}, u32[]{:S(2)}) async-start(bf16[64,64,128]{2,1,0:T(8,128)(2,1)} %back_hops.1), calls=%async_computation.3 | async-start | bytes 2097152 | tf_op jit(solution)/shard_map/all_to_all | solution.py:282
  277.8 16.1 %copy-start.8 = (bf16[64,64,128]{2,1,0:T(8,128)(2,1)S(1)}, bf16[64,64,128]{2,1,0:T(8,128)(2,1)}, u32[]{:S(2)}) copy-start(bf16[64,64,128]{2,1,0:T(8,128)(2,1)} %param.15) | copy-start | bytes 3145732
  277.8 1.0 copy-start.9
  278.8 67.6 %all-to-all-start.4 = ((bf16[64,64,128]{2,1,0:T(8,128)(2,1)}), bf16[64,64,128]{2,1,0:T(8,128)(2,1)S(1)}, u32[]{:S(2)}, u32[]{:S(2)}) async-start(bf16[64,64,128]{2,1,0:T(8,128)(2,1)} %forward_hops.1), calls=%async_computation.4 | async-start | bytes 2097152 | tf_op jit(solution)/shard_map/all_to_all | solution.py:282
  299.3 2.8 copy-start.5
  299.7 5.5 %collective-permute-start.1 = (bf16[64,8,128]{2,1,0:T(8,128)(2,1)S(1)}, bf16[64,8,128]{2,1,0:T(8,128)(2,1)S(1)}, u32[]{:S(2)}, u32[]{:S(2)}) collective-permute-start(bf16[64,8,128]{2,1,0:T(8,128)(2,1)S(1)} %slice.87), channel_id=1, source_target_pairs={{1,0},{2,1},{3,2},{4,3},{5,4},{6,5},{7,6},{9,8},{10,9},{11,10},{12... | collective-permute-start | bytes 393224 | tf_op jit(solution)/shard_map/ppermute | solution.py:23
Sparse Core Ops, SparseCore 0:
  68.7 32.2 all-gather.2

commit v3 on v2

--- a/solution.py
+++ b/solution.py
@@ -107,23 +107,22 @@
 def tables_kernel(slots, group, graph_ref, asked_ref, table_ref, pick_ref):
     rows, sensors = table_ref.shape[1:]
     places = rows - sensors
-    chunk = 64
+    chunk = 128
     for i in range(group):
         per_share = graph_ref.shape[2]
-        codes = [graph_ref[j // per_share, i, j % per_share : j % per_share + 1, :].astype(jnp.float32) for j in range(slots)]
-        weights = [
-            graph_ref[(slots + j) // per_share, i, j % per_share : j % per_share + 1, :].astype(jnp.float32)
-            for j in range(slots)
-        ]
+        codes = [graph_ref[j // per_share, i, j % per_share : j % per_share + 1, :] for j in range(slots)]
+        weights = [graph_ref[(slots + j) // per_share, i, j % per_share : j % per_share + 1, :] for j in range(slots)]
         for start in range(0, rows, chunk):
             ids = lax.broadcasted_iota(jnp.int32, (chunk, sensors), 0).astype(jnp.float32) + (start - rows // 2)
-            total = jnp.zeros((chunk, sensors), jnp.float32)
+            ids = ids.astype(jnp.bfloat16)
+            total = jnp.zeros((chunk, sensors), jnp.bfloat16)
             for j in range(slots):
                 total = jnp.where(ids == codes[j], weights[j], total)
-            table_ref[i, start : start + chunk, :] = total.astype(jnp.bfloat16)
-        own_ids = lax.broadcasted_iota(jnp.int32, (sensors, places), 0).astype(jnp.float32)
-        asked = asked_ref[i : i + 1, :]
-        pick_ref[i] = jnp.where(own_ids == asked, 1.0, 0.0).astype(jnp.bfloat16)
+            table_ref[i, start : start + chunk, :] = total
+        own_ids = lax.broadcasted_iota(jnp.int32, (sensors, places), 0).astype(jnp.float32).astype(jnp.bfloat16)
+        asked = asked_ref[i : i + 1, :].astype(jnp.bfloat16)
+        one = jnp.ones((sensors, places), jnp.bfloat16)
+        pick_ref[i] = jnp.where(own_ids == asked, one, jnp.zeros_like(one))
 
 
 def all_tables(slots, graph, asked):
@@ -165,20 +164,20 @@
 def back_kernel(places, grad_ref, weight_ref, table_ref, pick_ref, out_ref, base, second, first, gathered):
     peers, channels, sensors = grad_ref.shape
 
-    @pl.loop(0, peers)
+    @pl.loop(0, peers, unroll=8)
     def _(p):
         theta = t_mm(grad_ref[p], weight_ref[...])
         base[p] = theta[:, :LANES]
         second[p] = theta[:, LANES:].astype(jnp.bfloat16)
 
     def hop(source, finish):
-        @pl.loop(0, peers // 2)
+        @pl.loop(0, peers // 2, unroll=4)
         def _(pair):
             left = mm(table_ref[2 * pair, :places, :], source[2 * pair])
             right = mm(table_ref[2 * pair + 1, :places, :], source[2 * pair + 1])
             swap_places(gathered, pair, left, right)
 
-        @pl.loop(0, peers // 2)
+        @pl.loop(0, peers // 2, unroll=4)
         def _(pair):
             for side in range(2):
                 p = 2 * pair + side
@@ -198,18 +197,18 @@
 def forward_kernel(places, hidden_ref, unit_ref, one_ref, two_ref, table_ref, pick_ref, out_ref, start, middle, gathered):
     peers, channels, sensors = hidden_ref.shape
 
-    @pl.loop(0, peers)
+    @pl.loop(0, peers, unroll=8)
     def _(p):
         start[p] = t_mm(hidden_ref[p], unit_ref[...]).astype(jnp.bfloat16)
 
     def hop(source, finish):
-        @pl.loop(0, peers // 2)
+        @pl.loop(0, peers // 2, unroll=4)
         def _(pair):
             left = t_mm(pick_ref[2 * pair], source[2 * pair])
             right = t_mm(pick_ref[2 * pair + 1], source[2 * pair + 1])
             swap_places(gathered, pair, left, right)
 
-        @pl.loop(0, peers // 2)
+        @pl.loop(0, peers // 2, unroll=4)
         def _(pair):
             for side in range(2):
                 p = 2 * pair + side
@@ -284,7 +283,9 @@
 
 def asked_of(graph, slots, peer_count):
     sensors = graph.shape[3]
-    rows = graph[2 * slots // SHARE, :, : peer_count * CAPACITY // sensors, :]
+    per_share = graph.shape[2]
+    at = 2 * slots % per_share
+    rows = graph[2 * slots // per_share, :, at : at + peer_count * CAPACITY // sensors, :]
     rows = rows.reshape(peer_count, peer_count, CAPACITY).transpose(1, 0, 2)
     return rows.reshape(peer_count, peer_count * CAPACITY).astype(jnp.float32)
 

time: 358 us -> 303 us (0.85)
  Pallas kernels: 137 us -> 62.2 us
  waiting for transfers between devices: 105 us -> 142 us
  starting transfers between devices: 64.2 us -> 45.5 us
    all_to_all x5, waiting for transfers between devices: 100 us -> 138 us  [exchange(): lax.all_to_all(blocks, 'sensor', split_axis=0, concat_axis=0, tiled=True)]
    pallas_call x1, Pallas kernels: 53.1 us -> 25.9 us  [forward_hops(): pl.pallas_call(functools.partial(forward_kernel, places), out_shape=jax.S...]
    pallas_call x1, Pallas kernels: 44.3 us -> 18.9 us  [back_hops(): pl.pallas_call(functools.partial(back_kernel, places), out_shape=jax.Shap...]
    pallas_call x1, Pallas kernels: 37.8 us -> 15.8 us  [all_tables(): pl.pallas_call(functools.partial(tables_kernel, slots, group), grid=(peer...]
    all_to_all x5, starting transfers between devices: 59.8 us -> 41.3 us  [exchange(): lax.all_to_all(blocks, 'sensor', split_axis=0, concat_axis=0, tiled=True)]
  transfers between devices with their start and end apart: 8 -> 8, of which waited for: 4 -> 6; matrix products, arithmetic and copies ran while one was open for 6% -> 8% of each run, Pallas kernels for 38% -> 20%
where the time goes in v3:
time: 303 us; the launch traced here: 302 us
  waiting for transfers between devices  142 us (47%)
  Pallas kernels  62.2 us (21%)
  starting transfers between devices  45.5 us (15%)
  local copies, waits for them, and re-layouts  16.9 us (6%)
  between operations  14.4 us (5%)
  matrix products  11.3 us (4%)
  other arithmetic  9.09 us (3%)
    all_to_all x5, waiting for transfers between devices, exchange(): lax.all_to_all(blocks, 'sensor', split_axis=0, concat_axis=0, tiled=True)  138 us
    all_to_all x5, starting transfers between devices, exchange(): lax.all_to_all(blocks, 'sensor', split_axis=0, concat_axis=0, tiled=True)  41.3 us
    pallas_call x1, Pallas kernels, forward_hops(): pl.pallas_call(functools.partial(forward_kernel, places), out_shape=jax.S...  25.9 us
    pallas_call x1, Pallas kernels, back_hops(): pl.pallas_call(functools.partial(back_kernel, places), out_shape=jax.Shap...  18.9 us
    pallas_call x1, Pallas kernels, all_tables(): pl.pallas_call(functools.partial(tables_kernel, slots, group), grid=(peer...  15.8 us
    unnamed x33, local copies, waits for them, and re-layouts  14 us
    dot_general x2, matrix products, mm(): return jnp.dot(left, right, preferred_element_type=jnp.float32)  6.27 us
  transfers between devices with their start and end apart: 8, of which 6 were waited for; matrix products, arithmetic and copies ran while one was open for 8% of the time, Pallas kernels for 20%

profile of v3, /device:TPU:6, one launch (start us, length us, event | category | flops | bytes accessed | tf_op | source)
XLA Modules:
  0.0 301.6 jit_solution(9152121469622538464)
XLA Ops:
  7.2 0.0 copy-start
  7.2 0.8 copy.42.index_ref
  8.0 0.8 copy.43.weight_ref
  8.8 0.0 copy-start.4
  8.8 0.6 copy-done.4
  9.5 1.5 own_graph.1
  11.0 0.7 broadcast_in_dim.2
  11.8 18.7 %all-to-all-start = ((bf16[64,16,128]{2,1,0:T(8,128)(2,1)}), bf16[64,16,128]{2,1,0:T(8,128)(2,1)S(1)}, u32[]{:S(2)}, u32[]{:S(2)}) async-start(bf16[64,16,128]{2,1,0:T(8,128)(2,1)} %broadcast_in_dim.2), calls=%async_computation | async-start | bytes 524288 | tf_op jit(solution)/shard_map/all_to_all | solution.py:281
  30.5 0.0 copy-done.7
  30.5 0.0 copy-start.6
  30.5 1.6 copy.71
  32.2 20.8 %all-to-all-done = bf16[64,16,128]{2,1,0:T(8,128)(2,1)S(1)} async-done(((bf16[64,16,128]{2,1,0:T(8,128)(2,1)}), bf16[64,16,128]{2,1,0:T(8,128)(2,1)S(1)}, u32[]{:S(2)}, u32[]{:S(2)}) %all-to-all-start) | async-done | bytes 262176 | tf_op jit(solution)/shard_map/all_to_all | solution.py:281
  53.0 5.1 %all-to-all-start.1 = ((bf16[64,64,128]{2,1,0:T(8,128)(2,1)}), bf16[64,64,128]{2,1,0:T(8,128)(2,1)S(1)}, u32[]{:S(2)}, u32[]{:S(2)}) async-start(bf16[64,64,128]{2,1,0:T(8,128)(2,1)} %bitcast.68), calls=%async_computation.1 | async-start | bytes 2097152 | tf_op jit(solution)/shard_map/all_to_all | solution.py:281
  58.1 0.0 all-gather.3.cloned.1.call-start
  58.1 0.0 copy-done.6
  58.2 1.9 collective-permute-start
  60.1 0.0 copy-done.10
  60.1 0.0 copy-start.12
  60.1 4.3 %collective-permute-done = bf16[64,8,128]{2,1,0:T(8,128)(2,1)S(1)} collective-permute-done((bf16[64,8,128]{2,1,0:T(8,128)(2,1)S(1)}, bf16[64,8,128]{2,1,0:T(8,128)(2,1)S(1)}, u32[]{:S(2)}, u32[]{:S(2)}) %collective-permute-start) | collective-permute-done | bytes 131104 | tf_op jit(solution)/shard_map/ppermute | solution.py:23
  64.5 0.0 slice-done
  64.5 0.3 pad_maximum_fusion
  64.8 0.0 copy-done
  64.8 0.0 copy-done.12
  64.8 3.8 %fusion = f32[128,8192]{1,0:T(8,128)} fusion(bf16[128,128]{1,0:T(8,128)(2,1)S(1)} %copy-done, bf16[16,8,64,128]{3,2,1,0:T(8,128)(2,1)S(1)} %bitcast.65, f32[128]{0:T(128)S(1)} %copy-done.12), kind=kOutput, calls=%fused_computation.1 | convolution fusion | flops 269484032 | bytes 6324736 | tf_op jit(solution)/shard_map/dot_general | solution.py:27
  68.5 0.0 all-gather.3.cloned.1.call-update
  68.6 4.0 %bitcast_bitcast_fusion = bf16[64,64,128]{2,1,0:T(8,128)(2,1)} fusion(f32[128,8192]{1,0:T(8,128)} %fusion), kind=kLoop, calls=%fused_computation.30 | loop fusion | flops 2621440 | bytes 5242880 | tf_op jit(solution)/shard_map/transpose | solution.py:328
  72.6 39.9 %all-to-all-done.1.grad_ref = bf16[64,64,128]{2,1,0:T(8,128)(2,1)S(1)} async-done(((bf16[64,64,128]{2,1,0:T(8,128)(2,1)}), bf16[64,64,128]{2,1,0:T(8,128)(2,1)S(1)}, u32[]{:S(2)}, u32[]{:S(2)}) %all-to-all-start.1) | async-done | bytes 1048608 | tf_op jit(solution)/shard_map/all_to_all | solution.py:281
  112.5 5.8 %all-to-all-start.2 = ((bf16[64,64,128]{2,1,0:T(8,128)(2,1)}), bf16[64,64,128]{2,1,0:T(8,128)(2,1)S(1)}, u32[]{:S(2)}, u32[]{:S(2)}) async-start(bf16[64,64,128]{2,1,0:T(8,128)(2,1)} %bitcast_bitcast_fusion), calls=%async_computation.2 | async-start | bytes 2097152 | tf_op jit(solution)/shard_map/all_to_all | solution.py:281
  118.3 0.0 copy-done.11
  118.4 0.1 fusion.18
  118.5 0.0 all-gather.3.cloned.1.call-done
  118.5 0.9 slice_convert_fusion.1
  119.4 0.1 copy.44
  119.5 0.8 copy.45
  120.3 1.0 copy.46.asked_ref
  121.3 0.0 copy-start.3
  121.3 1.6 copy-done.3
  122.9 15.8 %all_tables.1 = (bf16[64,384,128]{2,1,0:T(8,128)(2,1)S(1)}, bf16[64,128,256]{2,1,0:T(8,128)(2,1)S(1)}) custom-call(bf16[8,64,16,128]{3,2,1,0:T(8,128)(2,1)S(1)} %bitcast.63, f32[64,256]{1,0:T(8,128)S(1)} %copy.46.asked_ref), custom_call_target="tpu_custom_call" | custom-call | flops 200000000 | bytes 12000000 | tf_op jit(solution)/shard_map/all_tables/pallas_call | solution.py:132
  138.7 0.0 copy-start.1
  138.7 2.6 copy-done.1
  141.3 2.0 copy-done.2
  143.4 18.9 %back_hops.1 = bf16[64,64,128]{2,1,0:T(8,128)(2,1)} custom-call(bf16[64,64,128]{2,1,0:T(8,128)(2,1)S(1)} %all-to-all-done.1.grad_ref, bf16[64,256]{1,0:T(8,128)(2,1)S(1)} %pad_maximum_fusion.1.weight_ref, bf16[64,384,128]{2,1,0:T(8,128)(2,1)} %copy-done.1, bf16[64,128,256]{2,1,0:T(8,128)(2,1)} %copy-done.2), custom_call_target="tpu_custom_call" | custom-call | flops 3000000000 | bytes 12000000 | tf_op jit(solution)/shard_map/back_hops/pallas_call | solution.py:239
  162.3 9.6 %all-to-all-done.2.hidden_ref = bf16[64,64,128]{2,1,0:T(8,128)(2,1)S(1)} async-done(((bf16[64,64,128]{2,1,0:T(8,128)(2,1)}), bf16[64,64,128]{2,1,0:T(8,128)(2,1)S(1)}, u32[]{:S(2)}, u32[]{:S(2)}) %all-to-all-start.2) | async-done | bytes 1048608 | tf_op jit(solution)/shard_map/all_to_all | solution.py:281
  171.9 5.8 %all-to-all-start.3 = ((bf16[64,64,128]{2,1,0:T(8,128)(2,1)}), bf16[64,64,128]{2,1,0:T(8,128)(2,1)S(1)}, u32[]{:S(2)}, u32[]{:S(2)}) async-start(bf16[64,64,128]{2,1,0:T(8,128)(2,1)} %back_hops.1), calls=%async_computation.3 | async-start | bytes 2097152 | tf_op jit(solution)/shard_map/all_to_all | solution.py:281
  177.8 25.9 %forward_hops.1 = bf16[64,64,128]{2,1,0:T(8,128)(2,1)} custom-call(bf16[64,64,128]{2,1,0:T(8,128)(2,1)S(1)} %all-to-all-done.2.hidden_ref, bf16[64,128]{1,0:T(8,128)(2,1)S(1)} %pad_convert_fusion.unit_ref, bf16[64,128]{1,0:T(8,128)(2,1)S(1)} %pad.16.one_ref, bf16[64,128]{1,0:T(8,128)(2,1)S(1)} %pad.17.two_ref, bf16[64,384,128]{2,1,0:T(8,128)(2,1)} %copy-done.1, ...), custom_call_target="tpu_custom_call" | custom-call | flops 3000000000 | bytes 12000000 | tf_op jit(solution)/shard_map/forward_hops/pallas_call | solution.py:262
  203.8 27.1 %all-to-all-done.3 = bf16[64,64,128]{2,1,0:T(8,128)(2,1)S(1)} async-done(((bf16[64,64,128]{2,1,0:T(8,128)(2,1)}), bf16[64,64,128]{2,1,0:T(8,128)(2,1)S(1)}, u32[]{:S(2)}, u32[]{:S(2)}) %all-to-all-start.3) | async-done | bytes 1048608 | tf_op jit(solution)/shard_map/all_to_all | solution.py:281
  230.9 1.0 copy-done.9
  231.9 5.8 %all-to-all-start.4 = ((bf16[64,64,128]{2,1,0:T(8,128)(2,1)}), bf16[64,64,128]{2,1,0:T(8,128)(2,1)S(1)}, u32[]{:S(2)}, u32[]{:S(2)}) async-start(bf16[64,64,128]{2,1,0:T(8,128)(2,1)} %forward_hops.1), calls=%async_computation.4 | async-start | bytes 2097152 | tf_op jit(solution)/shard_map/all_to_all | solution.py:281
  237.7 0.0 copy-done.8
  237.7 4.2 %multiply_convert_fusion.1 = (bf16[64,8192]{1,0:T(8,128)(2,1)S(1)}, bf16[64,8192]{1,0:T(8,128)(2,1)S(1)}) fusion(f32[128,8192]{1,0:T(8,128)} %fusion, bf16[8,8,64,128]{3,2,1,0:T(8,128)(2,1)S(1)} %bitcast.69, bf16[64,192]{1,0:T(8,128)(2,1)S(1)} %copy-done.11, bf16[64,64,128]{2,1,0:T(8,128)(2,1)} %copy-done.9), kind=kOutput, calls=%fused_computation.25 | convolution fusion | flops 74973184 | bytes 8404992 | tf_op jit(solution)/shard_map/dot_general | solution.py:334
  241.9 0.7 convolution_bitcast_fusion
  242.7 0.4 slice_bitcast_fusion
  243.1 0.0 copy-start.5
  243.1 0.4 copy.55
  243.5 2.2 collective-permute-start.1
  245.7 0.0 copy-done.5
  245.7 2.5 convolution_bitcast_fusion.1
  248.2 0.2 slice.57
  248.4 0.4 copy.54
  248.8 0.0 collective-permute-done.1
  248.8 1.4 fusion.2
  250.2 40.5 %all-to-all-done.4 = bf16[64,64,128]{2,1,0:T(8,128)(2,1)S(1)} async-done(((bf16[64,64,128]{2,1,0:T(8,128)(2,1)}), bf16[64,64,128]{2,1,0:T(8,128)(2,1)S(1)}, u32[]{:S(2)}, u32[]{:S(2)}) %all-to-all-start.4) | async-done | bytes 1048608 | tf_op jit(solution)/shard_map/all_to_all | solution.py:281
  290.7 2.4 fusion.6
  293.1 1.6 copy.48
  (16 shorter events, 0.2 us)
Async XLA Ops:
  7.2 57.6 %copy-start = (bf16[128,128]{1,0:T(8,128)(2,1)S(1)}, bf16[128,128]{1,0:T(8,128)(2,1)}, u32[]{:S(2)}) copy-start(bf16[128,128]{1,0:T(8,128)(2,1)} %param.9) | copy-start | bytes 98308
  8.8 0.7 copy-start.4
  9.5 21.0 %copy-start.7 = (bf16[64,64,128]{2,1,0:T(8,128)(2,1)S(1)}, bf16[64,64,128]{2,1,0:T(8,128)(2,1)}, u32[]{:S(2)}) copy-start(bf16[64,64,128]{2,1,0:T(8,128)(2,1)} %param.15) | copy-start | bytes 3145732
  11.8 41.2 %all-to-all-start = ((bf16[64,16,128]{2,1,0:T(8,128)(2,1)}), bf16[64,16,128]{2,1,0:T(8,128)(2,1)S(1)}, u32[]{:S(2)}, u32[]{:S(2)}) async-start(bf16[64,16,128]{2,1,0:T(8,128)(2,1)} %broadcast_in_dim.2), calls=%async_computation | async-start | bytes 524288 | tf_op jit(solution)/shard_map/all_to_all | solution.py:281
  30.5 27.6 %copy-start.6 = (bf16[64,64,128]{2,1,0:T(8,128)(2,1)S(1)}, bf16[64,64,128]{2,1,0:T(8,128)(2,1)}, u32[]{:S(2)}) copy-start(bf16[64,64,128]{2,1,0:T(8,128)(2,1)} %param.8) | copy-start | bytes 3145732
  53.0 7.1 %copy-start.10 = (bf16[64,16,128]{2,1,0:T(8,128)(2,1)}, bf16[64,16,128]{2,1,0:T(8,128)(2,1)S(1)}, u32[]{:S(2)}) copy-start(bf16[64,16,128]{2,1,0:T(8,128)(2,1)S(1)} %all-to-all-done) | copy-start | bytes 786436
  53.0 11.5 %slice-start = ((bf16[64,64,128]{2,1,0:T(8,128)(2,1)}), bf16[64,56,128]{2,1,0:T(8,128)(2,1)S(1)}, s32[]{:S(2)}) async-start(bf16[64,64,128]{2,1,0:T(8,128)(2,1)} %param.8), calls=%async_computation.6 | async-start | bytes 1835008 | tf_op jit(solution)/shard_map/slice | solution.py:319
  53.0 59.5 %all-to-all-start.1 = ((bf16[64,64,128]{2,1,0:T(8,128)(2,1)}), bf16[64,64,128]{2,1,0:T(8,128)(2,1)S(1)}, u32[]{:S(2)}, u32[]{:S(2)}) async-start(bf16[64,64,128]{2,1,0:T(8,128)(2,1)} %bitcast.68), calls=%async_computation.1 | async-start | bytes 2097152 | tf_op jit(solution)/shard_map/all_to_all | solution.py:281
  58.1 60.4 %all-gather.3.cloned.1.call-start = ((), (), s32[]{:S(2)}) async-start(), calls=%async_computation.5 | async-start | bytes 2359296 | tf_op jit(solution)/shard_map/all_gather | solution.py:314
  58.2 6.3 %collective-permute-start = (bf16[64,8,128]{2,1,0:T(8,128)(2,1)S(1)}, bf16[64,8,128]{2,1,0:T(8,128)(2,1)S(1)}, u32[]{:S(2)}, u32[]{:S(2)}) collective-permute-start(bf16[64,8,128]{2,1,0:T(8,128)(2,1)S(1)} %slice.40), channel_id=1, source_target_pairs={{0,1},{1,2},{2,3},{3,4},{4,5},{5,6},{6,7},{8,9},{9,10},{10,11},{11... | collective-permute-start | bytes 393224 | tf_op jit(solution)/shard_map/ppermute | solution.py:23
  60.1 4.7 %copy-start.12 = (f32[128]{0:T(128)S(1)}, f32[128]{0:T(128)}, u32[]{:S(2)}) copy-start(f32[128]{0:T(128)} %param.10) | copy-start | bytes 1540
  72.6 45.8 %copy-start.11 = (bf16[64,192]{1,0:T(8,128)(2,1)S(1)}, bf16[64,192]{1,0:T(8,128)(2,1)}, u32[]{:S(2)}) copy-start(bf16[64,192]{1,0:T(8,128)(2,1)} %param.11) | copy-start | bytes 73732
  112.5 59.4 %all-to-all-start.2 = ((bf16[64,64,128]{2,1,0:T(8,128)(2,1)}), bf16[64,64,128]{2,1,0:T(8,128)(2,1)S(1)}, u32[]{:S(2)}, u32[]{:S(2)}) async-start(bf16[64,64,128]{2,1,0:T(8,128)(2,1)} %bitcast_bitcast_fusion), calls=%async_computation.2 | async-start | bytes 2097152 | tf_op jit(solution)/shard_map/all_to_all | solution.py:281
  121.3 1.6 copy-start.3
  138.7 2.6 copy-start.1
  141.3 2.0 copy-start.2
  171.9 59.0 %all-to-all-start.3 = ((bf16[64,64,128]{2,1,0:T(8,128)(2,1)}), bf16[64,64,128]{2,1,0:T(8,128)(2,1)S(1)}, u32[]{:S(2)}, u32[]{:S(2)}) async-start(bf16[64,64,128]{2,1,0:T(8,128)(2,1)} %back_hops.1), calls=%async_computation.3 | async-start | bytes 2097152 | tf_op jit(solution)/shard_map/all_to_all | solution.py:281
  203.8 33.9 %copy-start.8 = (bf16[64,64,128]{2,1,0:T(8,128)(2,1)S(1)}, bf16[64,64,128]{2,1,0:T(8,128)(2,1)}, u32[]{:S(2)}) copy-start(bf16[64,64,128]{2,1,0:T(8,128)(2,1)} %param.15) | copy-start | bytes 3145732
  230.9 1.0 copy-start.9
  231.9 58.9 %all-to-all-start.4 = ((bf16[64,64,128]{2,1,0:T(8,128)(2,1)}), bf16[64,64,128]{2,1,0:T(8,128)(2,1)S(1)}, u32[]{:S(2)}, u32[]{:S(2)}) async-start(bf16[64,64,128]{2,1,0:T(8,128)(2,1)} %forward_hops.1), calls=%async_computation.4 | async-start | bytes 2097152 | tf_op jit(solution)/shard_map/all_to_all | solution.py:281
  243.1 2.6 copy-start.5
  243.5 5.3 %collective-permute-start.1 = (bf16[64,8,128]{2,1,0:T(8,128)(2,1)S(1)}, bf16[64,8,128]{2,1,0:T(8,128)(2,1)S(1)}, u32[]{:S(2)}, u32[]{:S(2)}) collective-permute-start(bf16[64,8,128]{2,1,0:T(8,128)(2,1)S(1)} %slice.87), channel_id=1, source_target_pairs={{1,0},{2,1},{3,2},{4,3},{5,4},{6,5},{7,6},{9,8},{10,9},{11,10},{12... | collective-permute-start | bytes 393224 | tf_op jit(solution)/shard_map/ppermute | solution.py:23
Sparse Core Ops, SparseCore 0:
  68.7 32.2 all-gather.2

commit v4 on v3

--- a/solution.py
+++ b/solution.py
@@ -10,7 +10,7 @@
 DILATION = 8
 CAPACITY = 4
 LANES = 128
-SHARE = 16
+SUBLANES = 8
 
 ROWS_BY_ROWS = (((1,), (1,)), ((), ()))
 COLUMNS_BY_COLUMNS = (((0,), (0,)), ((), ()))
@@ -35,14 +35,14 @@
     return lax.dot_general(left, right, COLUMNS_BY_COLUMNS, preferred_element_type=jnp.float32)
 
 
-def graph_kernel(peers, me_ref, index_ref, count_ref, weight_ref, graph_ref, member_all, owner_all):
-    sensors, slots = index_ref.shape
+def graph_kernel(peers, me_ref, index_ref, count_ref, weight_ref, graph_ref, member_all, owner_all, rows_all):
+    slots, sensors = index_ref.shape
     places = peers * CAPACITY
     half = (places + sensors) // 2
     me = me_ref[0]
-    index = index_ref[...].T
+    index = index_ref[...]
     live = lax.broadcasted_iota(jnp.int32, (slots, sensors), 0) < count_ref[...]
-    masked = jnp.where(live, weight_ref[...].T, 0.0)
+    masked = jnp.where(live, weight_ref[...], 0.0)
     trans = masked / jnp.sum(masked, axis=0, keepdims=True)
     owner = jnp.where(live, index // sensors, -1)
     member = index % sensors
@@ -68,86 +68,81 @@
     distant = owner * CAPACITY + ranks.astype(jnp.int32)
     row = jnp.where(owner == me, places + member, distant) - half
     row = jnp.where(live, row, half)
-    graph_ref[...] = jnp.zeros(graph_ref.shape, jnp.bfloat16)
-    graph_ref[0:slots, :] = row.astype(jnp.float32).astype(jnp.bfloat16)
-    graph_ref[slots : 2 * slots, :] = trans.astype(jnp.bfloat16)
+    row = row.astype(jnp.float32)
+    trans = trans.astype(jnp.bfloat16).astype(jnp.float32)
+    part = SUBLANES // 2
+    for i in range(slots // part):
+        rows_all[i] = jnp.concatenate([row[i * part : (i + 1) * part], trans[i * part : (i + 1) * part]], axis=0)
     expand = lax.broadcasted_iota(jnp.int32, (places, peers), 0) // CAPACITY == lax.broadcasted_iota(
         jnp.int32, (places, peers), 1
     )
     spread_rank = mm(jnp.where(expand, 1.0, 0.0).astype(jnp.bfloat16), spread_rank)
     wanted_rank = (lax.broadcasted_iota(jnp.int32, (places, sensors), 0) % CAPACITY).astype(jnp.float32)
     chosen = jnp.where(spread_rank == wanted_rank, 1.0, 0.0).astype(jnp.bfloat16)
-    lane_ids = lax.broadcasted_iota(jnp.int32, (SHARE, sensors), 1).astype(jnp.float32)
-    first_row = lax.broadcasted_iota(jnp.int32, (SHARE, sensors), 0) == 0
+    lane_ids = lax.broadcasted_iota(jnp.int32, (SUBLANES, sensors), 1).astype(jnp.float32)
+    first_row = lax.broadcasted_iota(jnp.int32, (SUBLANES, sensors), 0) == 0
     label = jnp.where(first_row, lane_ids, 1.0).astype(jnp.bfloat16)
     asked = mm_t(label, chosen)
     asked = jnp.where(asked[1:2] > 0.5, asked[0:1], -1.0)
-    asked = jnp.concatenate([asked[:, i * sensors : (i + 1) * sensors] for i in range(places // sensors)], axis=0)
-    asked = jnp.concatenate([asked, jnp.zeros((SHARE - asked.shape[0], sensors), jnp.float32)], axis=0)
-    graph_ref[2 * slots : 2 * slots + SHARE, :] = asked.astype(jnp.bfloat16)
-
-
-def own_graph(peers, shares, myself, index, count, weight):
+    asked = [asked[:, i * sensors : (i + 1) * sensors] for i in range(places // sensors)]
+    asked.append(jnp.zeros((SUBLANES - len(asked), sensors), jnp.float32))
+    graph_ref[...] = jnp.concatenate([rows_all[me_ref[1]]] + asked, axis=0).astype(jnp.bfloat16)
+
+
+def own_graph(peers, myself, share, index, count, weight):
     sensors, slots = index.shape
     return pl.pallas_call(
         functools.partial(graph_kernel, peers),
-        out_shape=jax.ShapeDtypeStruct((shares * SHARE, sensors), jnp.bfloat16),
+        out_shape=jax.ShapeDtypeStruct((2 * SUBLANES, sensors), jnp.bfloat16),
         in_specs=[pl.BlockSpec(memory_space=pltpu.SMEM), VMEM, VMEM, VMEM],
         out_specs=VMEM,
         scratch_shapes=[
             pltpu.VMEM((sensors, slots * sensors), jnp.bfloat16),
             pltpu.VMEM((peers, slots * sensors), jnp.bfloat16),
+            pltpu.VMEM((2 * slots // SUBLANES, SUBLANES, sensors), jnp.float32),
         ],
         compiler_params=pltpu.CompilerParams(vmem_limit_bytes=32 * 1024 * 1024),
         cost_estimate=pl.CostEstimate(flops=4 * 10**8, bytes_accessed=10**6, transcendentals=0),
         name="own_graph",
-    )(myself.reshape(1).astype(jnp.int32), index, count.reshape(1, sensors), weight)
-
-
-def tables_kernel(slots, group, graph_ref, asked_ref, table_ref, pick_ref):
+    )(jnp.stack([myself, share]).astype(jnp.int32), index.T, count.reshape(1, sensors), weight.T)
+
+
+def fill_tables(p, shares, asked_ref, table_ref, pick_ref):
     rows, sensors = table_ref.shape[1:]
     places = rows - sensors
+    part = SUBLANES // 2
     chunk = 128
-    for i in range(group):
-        per_share = graph_ref.shape[2]
-        codes = [graph_ref[j // per_share, i, j % per_share : j % per_share + 1, :] for j in range(slots)]
-        weights = [graph_ref[(slots + j) // per_share, i, j % per_share : j % per_share + 1, :] for j in range(slots)]
-        for start in range(0, rows, chunk):
-            ids = lax.broadcasted_iota(jnp.int32, (chunk, sensors), 0).astype(jnp.float32) + (start - rows // 2)
-            ids = ids.astype(jnp.bfloat16)
-            total = jnp.zeros((chunk, sensors), jnp.bfloat16)
-            for j in range(slots):
-                total = jnp.where(ids == codes[j], weights[j], total)
-            table_ref[i, start : start + chunk, :] = total
-        own_ids = lax.broadcasted_iota(jnp.int32, (sensors, places), 0).astype(jnp.float32).astype(jnp.bfloat16)
-        asked = asked_ref[i : i + 1, :].astype(jnp.bfloat16)
-        one = jnp.ones((sensors, places), jnp.bfloat16)
-        pick_ref[i] = jnp.where(own_ids == asked, one, jnp.zeros_like(one))
-
-
-def all_tables(slots, graph, asked):
-    shares, peers, per_share, sensors = graph.shape
-    places = asked.shape[1]
-    group = 8
-    return pl.pallas_call(
-        functools.partial(tables_kernel, slots, group),
-        grid=(peers // group,),
-        out_shape=(
-            jax.ShapeDtypeStruct((peers, places + sensors, sensors), jnp.bfloat16),
-            jax.ShapeDtypeStruct((peers, sensors, places), jnp.bfloat16),
-        ),
-        in_specs=[
-            pl.BlockSpec((shares, group, per_share, sensors), lambda i: (0, i, 0, 0)),
-            pl.BlockSpec((group, places), lambda i: (i, 0)),
-        ],
-        out_specs=(
-            pl.BlockSpec((group, places + sensors, sensors), lambda i: (i, 0, 0)),
-            pl.BlockSpec((group, sensors, places), lambda i: (i, 0, 0)),
-        ),
-        compiler_params=pltpu.CompilerParams(vmem_limit_bytes=32 * 1024 * 1024),
-        cost_estimate=pl.CostEstimate(flops=2 * 10**8, bytes_accessed=12 * 10**6, transcendentals=0),
-        name="all_tables",
-    )(graph, asked)
+    codes = [share[j : j + 1, :] for share in shares for j in range(part)]
+    weights = [share[part + j : part + j + 1, :] for share in shares for j in range(part)]
+    blocks = []
+    for start in range(0, rows, chunk):
+        ids = lax.broadcasted_iota(jnp.int32, (chunk, sensors), 0).astype(jnp.float32) + (start - rows // 2)
+        ids = ids.astype(jnp.bfloat16)
+        total = jnp.zeros((chunk, sensors), jnp.bfloat16)
+        for code, weight in zip(codes, weights):
+            total = jnp.where(ids == code, weight, total)
+        table_ref[p, start : start + chunk, :] = total
+        blocks.append(total)
+    own_ids = lax.broadcasted_iota(jnp.int32, (sensors, places), 0).astype(jnp.float32).astype(jnp.bfloat16)
+    asked = asked_ref[pl.ds(p, 1), :].astype(jnp.bfloat16)
+    one = jnp.ones((sensors, places), jnp.bfloat16)
+    pick_ref[p] = jnp.where(own_ids == asked, one, jnp.zeros_like(one))
+    return blocks[: places // chunk]
+
+
+def turn_requests(requests, asked_ref):
+    peers, sublanes, lanes = requests.shape
+    places = peers * CAPACITY
+    rows = lax.broadcasted_iota(jnp.int32, requests.shape, 1)
+    parts = [jnp.sum(jnp.where(rows == i, requests, 0.0), axis=1) for i in range(places // lanes)]
+    named = jnp.concatenate(parts, axis=1).astype(jnp.bfloat16)
+    peer_ids = lax.broadcasted_iota(jnp.int32, (peers, places), 0)
+    owner = lax.broadcasted_iota(jnp.int32, (peers, places), 1) // CAPACITY
+    belongs = jnp.where(peer_ids == owner, 1.0, 0.0).astype(jnp.bfloat16)
+    every = t_mm(named, belongs)
+    same = lax.broadcasted_iota(jnp.int32, (places, places), 0) % CAPACITY
+    same = same == lax.broadcasted_iota(jnp.int32, (places, places), 1) % CAPACITY
+    asked_ref[...] = mm(belongs, jnp.where(same, every, 0.0).astype(jnp.bfloat16))
 
 
 def swap_places(gathered, pair, left, right):
@@ -161,23 +156,31 @@
     gathered[:, 1, at, :] = odd.reshape(shape)
 
 
-def back_kernel(places, grad_ref, weight_ref, table_ref, pick_ref, out_ref, base, second, first, gathered):
-    peers, channels, sensors = grad_ref.shape
-
-    @pl.loop(0, peers, unroll=8)
-    def _(p):
-        theta = t_mm(grad_ref[p], weight_ref[...])
-        base[p] = theta[:, :LANES]
-        second[p] = theta[:, LANES:].astype(jnp.bfloat16)
-
-    def hop(source, finish):
-        @pl.loop(0, peers // 2, unroll=4)
-        def _(pair):
-            left = mm(table_ref[2 * pair, :places, :], source[2 * pair])
-            right = mm(table_ref[2 * pair + 1, :places, :], source[2 * pair + 1])
-            swap_places(gathered, pair, left, right)
-
-        @pl.loop(0, peers // 2, unroll=4)
+def back_kernel(
+    places, arrived_ref, near_ref, far_ref, weight_ref, out_ref, table_ref, pick_ref, base, second, first, gathered, asked
+):
+    peers, channels, sensors = out_ref.shape
+    start = channels + SUBLANES
+    turn_requests(arrived_ref[:, start : start + SUBLANES, :].astype(jnp.float32), asked)
+
+    @pl.loop(0, peers // 2, unroll=4)
+    def _(pair):
+        sent = []
+        for side in range(2):
+            p = 2 * pair + side
+            theta = t_mm(arrived_ref[p, :channels, :], weight_ref[...])
+            base[p] = theta[:, :LANES]
+            value = theta[:, LANES:].astype(jnp.bfloat16)
+            second[p] = value
+            shares = [arrived_ref[p, channels:start, :]]
+            shares += [near_ref[i, p] for i in range(near_ref.shape[0])]
+            shares += [far_ref[i, p] for i in range(far_ref.shape[0])]
+            blocks = fill_tables(p, shares, asked, table_ref, pick_ref)
+            sent.append(jnp.concatenate([mm(block, value) for block in blocks], axis=0))
+        swap_places(gathered, pair, *sent)
+
+    def absorb(source, finish):
+        @pl.loop(0, peers // 2, unroll=32)
         def _(pair):
             for side in range(2):
                 p = 2 * pair + side
@@ -190,25 +193,32 @@
     def keep_out(p, value):
         out_ref[p] = value.T[:channels].astype(jnp.bfloat16)
 
-    hop(second, keep_first)
-    hop(first, keep_out)
+    absorb(second, keep_first)
+
+    @pl.loop(0, peers // 2, unroll=32)
+    def _(pair):
+        left = mm(table_ref[2 * pair, :places, :], first[2 * pair])
+        right = mm(table_ref[2 * pair + 1, :places, :], first[2 * pair + 1])
+        swap_places(gathered, pair, left, right)
+
+    absorb(first, keep_out)
 
 
 def forward_kernel(places, hidden_ref, unit_ref, one_ref, two_ref, table_ref, pick_ref, out_ref, start, middle, gathered):
     peers, channels, sensors = hidden_ref.shape
 
-    @pl.loop(0, peers, unroll=8)
+    @pl.loop(0, peers, unroll=32)
     def _(p):
         start[p] = t_mm(hidden_ref[p], unit_ref[...]).astype(jnp.bfloat16)
 
     def hop(source, finish):
-        @pl.loop(0, peers // 2, unroll=4)
+        @pl.loop(0, peers // 2, unroll=32)
         def _(pair):
             left = t_mm(pick_ref[2 * pair], source[2 * pair])
             right = t_mm(pick_ref[2 * pair + 1], source[2 * pair + 1])
             swap_places(gathered, pair, left, right)
 
-        @pl.loop(0, peers // 2, unroll=4)
+        @pl.loop(0, peers // 2, unroll=32)
         def _(pair):
             for side in range(2):
                 p = 2 * pair + side
@@ -230,27 +240,33 @@
     return jnp.pad(block, ((0, 0), (0, LANES - block.shape[1])))
 
 
-def back_hops(grad, diff_weight, table, pick):
-    peers, channels, sensors = grad.shape
-    places = pick.shape[2]
+def back_hops(arrived, near, far, diff_weight):
+    peers, _, sensors = arrived.shape
+    channels = diff_weight.shape[0]
+    places = peers * CAPACITY
     weight = jnp.concatenate(
         [to_lanes(diff_weight[:, channels : 2 * channels]), to_lanes(diff_weight[:, 2 * channels :])], axis=1
     )
     return pl.pallas_call(
         functools.partial(back_kernel, places),
-        out_shape=jax.ShapeDtypeStruct(grad.shape, jnp.bfloat16),
+        out_shape=(
+            jax.ShapeDtypeStruct((peers, channels, sensors), jnp.bfloat16),
+            jax.ShapeDtypeStruct((peers, places + sensors, sensors), jnp.bfloat16),
+            jax.ShapeDtypeStruct((peers, sensors, places), jnp.bfloat16),
+        ),
         in_specs=[VMEM] * 4,
-        out_specs=VMEM,
+        out_specs=(VMEM, VMEM, VMEM),
         scratch_shapes=[
             pltpu.VMEM((peers, sensors, LANES), jnp.float32),
             pltpu.VMEM((peers, sensors, LANES), jnp.bfloat16),
             pltpu.VMEM((peers, sensors, LANES), jnp.bfloat16),
             pltpu.VMEM((peers // 2, 2, peers * CAPACITY, LANES), jnp.float32),
+            pltpu.VMEM((peers, places), jnp.float32),
         ],
-        compiler_params=pltpu.CompilerParams(vmem_limit_bytes=48 * 1024 * 1024),
+        compiler_params=pltpu.CompilerParams(vmem_limit_bytes=56 * 1024 * 1024),
         cost_estimate=pl.CostEstimate(flops=3 * 10**9, bytes_accessed=12 * 10**6, transcendentals=0),
         name="back_hops",
-    )(grad, weight, table, pick)
+    )(arrived, near, far, weight)
 
 
 def forward_hops(hidden, diff_weight, table, pick):
@@ -281,15 +297,6 @@
     return lax.all_to_all(blocks, "sensor", split_axis=0, concat_axis=0, tiled=True)
 
 
-def asked_of(graph, slots, peer_count):
-    sensors = graph.shape[3]
-    per_share = graph.shape[2]
-    at = 2 * slots % per_share
-    rows = graph[2 * slots // per_share, :, at : at + peer_count * CAPACITY // sensors, :]
-    rows = rows.reshape(peer_count, peer_count, CAPACITY).transpose(1, 0, 2)
-    return rows.reshape(peer_count, peer_count * CAPACITY).astype(jnp.float32)
-
-
 def per_device(
     signal,
     conv_weight,
@@ -301,18 +308,25 @@
     cotangent,
 ):
     channels, step_count, sensor_count = signal.shape
-    slots = neighbour_index.shape[1]
     peer_count = lax.axis_size("sensor")
     share_count = lax.axis_size("tm")
 
     graph = own_graph(
-        peer_count, share_count, lax.axis_index("sensor"), neighbour_index, neighbour_count, edge_weight
-    )
-    share = lax.dynamic_slice_in_dim(graph, lax.axis_index("tm") * SHARE, SHARE, 0)
-    share = exchange(jnp.broadcast_to(share[None], (peer_count, SHARE, sensor_count)))
-    grad_in = exchange(cotangent.transpose(1, 0, 2), share)
-    graphs = lax.all_gather(share, "tm", axis=0, tiled=False)
-    table, pick = all_tables(slots, graphs, asked_of(graphs, slots, peer_count))
+        peer_count,
+        lax.axis_index("sensor"),
+        lax.axis_index("tm"),
+        neighbour_index,
+        neighbour_count,
+        edge_weight,
+    )
+    graph = jnp.broadcast_to(graph[None], (peer_count, 2 * SUBLANES, sensor_count))
+    arrived = exchange(jnp.concatenate([cotangent.transpose(1, 0, 2), graph], axis=1))
+    own = arrived[:, channels : channels + SUBLANES]
+    near = [
+        lax.ppermute(own, "tm", [(i, (i + by) % share_count) for i in range(share_count)])
+        for by in range(2, share_count, 2)
+    ]
+    far = lax.ppermute(jnp.stack([own] + near), "tm", [(i, i ^ 1) for i in range(share_count)])
 
     tail_steps = signal[:, step_count - DILATION :, :]
     before = from_behind(tail_steps, "tm", 1)
@@ -325,10 +339,11 @@
     gate_part = jax.nn.sigmoid(preact[channels:])
     hidden = (tanh_part * gate_part).astype(jnp.bfloat16)
     hidden_in = exchange(
-        hidden.reshape(channels, step_count, sensor_count).transpose(1, 0, 2), grad_in
-    )
-
-    grad_out = exchange(back_hops(grad_in, diff_weight, table, pick), hidden_in)
+        hidden.reshape(channels, step_count, sensor_count).transpose(1, 0, 2), arrived
+    )
+
+    back, table, pick = back_hops(arrived, jnp.stack(near), far, diff_weight)
+    grad_out = exchange(back, hidden_in)
     mixed_out = exchange(forward_hops(hidden_in, diff_weight, table, pick), grad_out)
 
     theta_back = lax.dot_general(

time: 303 us -> 281 us (0.927)
  Pallas kernels: 62.2 us -> 45.6 us
  between operations: 14.4 us -> 0.98 us
  starting transfers between devices: 45.5 us -> 54.1 us
  waiting for transfers between devices: 142 us -> 150 us
  local copies, waits for them, and re-layouts: 16.9 us -> 8.93 us
    ppermute x0 -> x4, starting transfers between devices: none -> 11.9 us  [the longest x3 9.76 us: per_device(): lax.ppermute(own, 'tm', [(i, (i + by) % share_count) for i in range(share...]
    pallas_call x2 -> x1, Pallas kernels: 34.7 us -> 26 us  [back_hops(): pl.pallas_call(functools.partial(back_kernel, places), out_shape=(jax.Sha...]
    pallas_call x1, Pallas kernels: 25.9 us -> 17.6 us  [forward_hops(): pl.pallas_call(functools.partial(forward_kernel, places), out_shape=jax.S...]
    unnamed x33 -> x27, local copies, waits for them, and re-layouts: 14 us -> 7.61 us
    all_to_all x5 -> x4, waiting for transfers between devices: 138 us -> 142 us  [exchange(): lax.all_to_all(blocks, 'sensor', split_axis=0, concat_axis=0, tiled=True)]
    all_to_all x5 -> x4, starting transfers between devices: 41.3 us -> 37.3 us  [exchange(): lax.all_to_all(blocks, 'sensor', split_axis=0, concat_axis=0, tiled=True)]
    ppermute x0 -> x4, waiting for transfers between devices: none -> 3.41 us  [the longest x3 3.23 us: per_device(): lax.ppermute(own, 'tm', [(i, (i + by) % share_count) for i in range(share...]
  transfers between devices with their start and end apart: 8 -> 10, of which waited for: 6 -> 8; matrix products, arithmetic and copies ran while one was open for 8% -> 6% of each run, Pallas kernels for 20% -> 16%
where the time goes in v4:
time: 281 us; the launch traced here: 277 us
  waiting for transfers between devices  150 us (53%)
  starting transfers between devices  54.1 us (19%)
  Pallas kernels  45.6 us (16%)
  matrix products  9.19 us (3%)
  local copies, waits for them, and re-layouts  8.93 us (3%)
  other arithmetic  8.62 us (3%)
    all_to_all x4, waiting for transfers between devices, exchange(): lax.all_to_all(blocks, 'sensor', split_axis=0, concat_axis=0, tiled=True)  142 us
    all_to_all x4, starting transfers between devices, exchange(): lax.all_to_all(blocks, 'sensor', split_axis=0, concat_axis=0, tiled=True)  37.3 us
    pallas_call x1, Pallas kernels, back_hops(): pl.pallas_call(functools.partial(back_kernel, places), out_shape=(jax.Sha...  26 us
    pallas_call x1, Pallas kernels, forward_hops(): pl.pallas_call(functools.partial(forward_kernel, places), out_shape=jax.S...  17.6 us
    ppermute x3, starting transfers between devices, per_device(): lax.ppermute(own, 'tm', [(i, (i + by) % share_count) for i in range(share...  9.76 us
    unnamed x27, local copies, waits for them, and re-layouts  7.61 us
  transfers between devices with their start and end apart: 10, of which 8 were waited for; matrix products, arithmetic and copies ran while one was open for 6% of the time, Pallas kernels for 16%

profile of v4, /device:TPU:6, one launch (start us, length us, event | category | flops | bytes accessed | tf_op | source)
XLA Modules:
  0.0 277.2 jit_solution(8365600104196841376)
XLA Ops:
  0.6 0.0 copy-start
  0.6 0.0 copy-start.2
  0.7 0.0 copy-start.3
  0.7 0.0 copy-start.1
  0.7 1.9 copy.41
  2.6 0.1 pad_add_fusion.me_ref
  2.7 0.0 copy-done.2
  2.7 0.0 copy-done.3
  2.7 0.0 copy-done.1
  2.7 1.9 own_graph.1
  4.6 0.1 broadcast_in_dim.2
  4.7 0.0 copy-start.6
  4.7 1.1 pad_maximum_fusion.1
  5.9 19.1 %all-to-all-start = ((bf16[64,80,128]{2,1,0:T(8,128)(2,1)}), bf16[64,80,128]{2,1,0:T(8,128)(2,1)}, u32[]{:S(2)}, u32[]{:S(2)}) async-start(bf16[64,80,128]{2,1,0:T(8,128)(2,1)} %pad_maximum_fusion.1), calls=%async_computation | async-start | bytes 2621440 | tf_op jit(solution)/shard_map/all_to_all | solution.py:297
  25.0 0.0 copy-done.6
  25.0 1.9 collective-permute-start
  26.9 0.0 copy-start.9
  27.0 4.3 %collective-permute-done = bf16[64,8,128]{2,1,0:T(8,128)(2,1)S(1)} collective-permute-done((bf16[64,8,128]{2,1,0:T(8,128)(2,1)S(1)}, bf16[64,8,128]{2,1,0:T(8,128)(2,1)S(1)}, u32[]{:S(2)}, u32[]{:S(2)}) %collective-permute-start) | collective-permute-done | bytes 131104 | tf_op jit(solution)/shard_map/ppermute | solution.py:23
  31.3 0.0 slice-done
  31.3 0.3 pad_maximum_fusion
  31.6 0.0 copy-done
  31.6 0.0 copy-done.9
  31.6 1.7 fusion
  33.3 0.0 copy-start.4
  33.3 2.1 copy-done.4
  35.4 1.8 bitcast_bitcast_fusion
  37.2 54.2 %all-to-all-done.arrived_ref = bf16[64,80,128]{2,1,0:T(8,128)(2,1)} async-done(((bf16[64,80,128]{2,1,0:T(8,128)(2,1)}), bf16[64,80,128]{2,1,0:T(8,128)(2,1)}, u32[]{:S(2)}, u32[]{:S(2)}) %all-to-all-start) | async-done | bytes 1310752 | tf_op jit(solution)/shard_map/all_to_all | solution.py:297
  91.4 5.8 %all-to-all-start.1 = ((bf16[64,64,128]{2,1,0:T(8,128)(2,1)}), bf16[64,64,128]{2,1,0:T(8,128)(2,1)S(1)}, u32[]{:S(2)}, u32[]{:S(2)}) async-start(bf16[64,64,128]{2,1,0:T(8,128)(2,1)} %bitcast_bitcast_fusion), calls=%async_computation.1 | async-start | bytes 2097152 | tf_op jit(solution)/shard_map/all_to_all | solution.py:297
  97.2 0.9 slice_bitcast_fusion.2
  98.1 2.7 collective-permute-start.3
  100.9 3.0 %collective-permute-start.2 = (bf16[64,8,128]{2,1,0:T(8,128)(2,1)S(1)}, bf16[64,8,128]{2,1,0:T(8,128)(2,1)S(1)}, u32[]{:S(2)}, u32[]{:S(2)}) collective-permute-start(bf16[64,8,128]{2,1,0:T(8,128)(2,1)S(1)} %get-tuple-element.23), channel_id=1, source_target_pairs={{0,4},{1,5},{2,6},{3,7},{4,0},{5,1},{6,2},{7,3},{8,12},{9,13},{10,... | collective-permute-start | bytes 393224 | tf_op jit(solution)/shard_map/ppermute | solution.py:326
  103.9 4.0 %collective-permute-start.1 = (bf16[64,8,128]{2,1,0:T(8,128)(2,1)S(1)}, bf16[64,8,128]{2,1,0:T(8,128)(2,1)S(1)}, u32[]{:S(2)}, u32[]{:S(2)}) collective-permute-start(bf16[64,8,128]{2,1,0:T(8,128)(2,1)S(1)} %get-tuple-element.23), channel_id=1, source_target_pairs={{0,2},{1,3},{2,4},{3,5},{4,6},{5,7},{6,0},{7,1},{8,10},{9,11},{10,... | collective-permute-start | bytes 393224 | tf_op jit(solution)/shard_map/ppermute | solution.py:326
  107.9 0.0 collective-permute-done.3
  107.9 1.3 collective-permute-done.2
  109.3 1.9 collective-permute-done.1
  111.2 0.1 pad_maximum_fusion.2
  111.2 2.1 collective-permute-start.4
  113.3 0.0 copy-done.8
  113.4 0.1 fusion.18
  113.5 0.6 pad_maximum_fusion.4.weight_ref
  114.1 0.8 pad_maximum_fusion.3.near_ref
  114.9 0.2 collective-permute-done.4.far_ref
  115.0 0.8 copy-done.10
  115.9 26.0 %back_hops.1 = (bf16[64,64,128]{2,1,0:T(8,128)(2,1)}, bf16[64,384,128]{2,1,0:T(8,128)(2,1)}, bf16[64,128,256]{2,1,0:T(8,128)(2,1)}) custom-call(bf16[64,80,128]{2,1,0:T(8,128)(2,1)} %all-to-all-done.arrived_ref, bf16[3,64,8,128]{3,2,1,0:T(8,128)(2,1)} %pad_maximum_fusion.3.near_ref, bf16[4,64,8,128]{3,2,1,0:T(8,128)(2,1)} %copy-done.10, ...), custom_call_target="tpu_custom_call" | custom-call | flops 3000000000 | bytes 12000000 | tf_op jit(solution)/shard_map/back_hops/pallas_call | solution.py:250
  141.9 9.8 %all-to-all-done.1.hidden_ref = bf16[64,64,128]{2,1,0:T(8,128)(2,1)S(1)} async-done(((bf16[64,64,128]{2,1,0:T(8,128)(2,1)}), bf16[64,64,128]{2,1,0:T(8,128)(2,1)S(1)}, u32[]{:S(2)}, u32[]{:S(2)}) %all-to-all-start.1) | async-done | bytes 1048608 | tf_op jit(solution)/shard_map/all_to_all | solution.py:297
  151.6 6.3 %all-to-all-start.2 = ((bf16[64,64,128]{2,1,0:T(8,128)(2,1)}), bf16[64,64,128]{2,1,0:T(8,128)(2,1)}, u32[]{:S(2)}, u32[]{:S(2)}) async-start(bf16[64,64,128]{2,1,0:T(8,128)(2,1)} %get-tuple-element.12), calls=%async_computation.2 | async-start | bytes 2097152 | tf_op jit(solution)/shard_map/all_to_all | solution.py:297
  158.0 17.6 %forward_hops.1 = bf16[64,64,128]{2,1,0:T(8,128)(2,1)} custom-call(bf16[64,64,128]{2,1,0:T(8,128)(2,1)S(1)} %all-to-all-done.1.hidden_ref, bf16[64,128]{1,0:T(8,128)(2,1)S(1)} %pad_convert_fusion.unit_ref, bf16[64,128]{1,0:T(8,128)(2,1)S(1)} %pad.16.one_ref, bf16[64,128]{1,0:T(8,128)(2,1)S(1)} %pad.17.two_ref, ...), custom_call_target="tpu_custom_call" | custom-call | flops 3000000000 | bytes 12000000 | tf_op jit(solution)/shard_map/forward_hops/pallas_call | solution.py:278
  175.6 37.0 %all-to-all-done.2 = bf16[64,64,128]{2,1,0:T(8,128)(2,1)} async-done(((bf16[64,64,128]{2,1,0:T(8,128)(2,1)}), bf16[64,64,128]{2,1,0:T(8,128)(2,1)}, u32[]{:S(2)}, u32[]{:S(2)}) %all-to-all-start.2) | async-done | bytes 1048608 | tf_op jit(solution)/shard_map/all_to_all | solution.py:297
  212.6 6.1 %all-to-all-start.3 = ((bf16[64,64,128]{2,1,0:T(8,128)(2,1)}), bf16[64,64,128]{2,1,0:T(8,128)(2,1)S(1)}, u32[]{:S(2)}, u32[]{:S(2)}) async-start(bf16[64,64,128]{2,1,0:T(8,128)(2,1)} %forward_hops.1), calls=%async_computation.3 | async-start | bytes 2097152 | tf_op jit(solution)/shard_map/all_to_all | solution.py:297
  218.7 0.0 copy-done.7
  218.7 4.2 %multiply_convert_fusion.1 = (bf16[64,8192]{1,0:T(8,128)(2,1)S(1)}, bf16[64,8192]{1,0:T(8,128)(2,1)S(1)}) fusion(f32[128,8192]{1,0:T(8,128)} %copy-done.4, bf16[8,8,64,128]{3,2,1,0:T(8,128)(2,1)S(1)} %bitcast.72, bf16[64,192]{1,0:T(8,128)(2,1)S(1)} %copy-done.8, bf16[64,64,128]{2,1,0:T(8,128)(2,1)} %all-to-all-done.2), kind=kOutput, calls=%fused_computation.25 | convolution fusion | flops 74973184 | bytes 8404992 | tf_op jit(solution)/shard_map/dot_general | solution.py:349
  223.0 0.7 convolution_bitcast_fusion
  223.7 0.4 slice_bitcast_fusion
  224.1 0.0 copy-start.5
  224.1 0.4 copy.25
  224.6 3.0 %collective-permute-start.5 = (bf16[64,8,128]{2,1,0:T(8,128)(2,1)S(1)}, bf16[64,8,128]{2,1,0:T(8,128)(2,1)S(1)}, u32[]{:S(2)}, u32[]{:S(2)}) collective-permute-start(bf16[64,8,128]{2,1,0:T(8,128)(2,1)S(1)} %slice.87), channel_id=1, source_target_pairs={{1,0},{2,1},{3,2},{4,3},{5,4},{6,5},{7,6},{9,8},{10,9},{11,10},{12... | collective-permute-start | bytes 393224 | tf_op jit(solution)/shard_map/ppermute | solution.py:23
  227.5 2.5 convolution_bitcast_fusion.1
  230.1 0.2 slice.57
  230.2 0.4 copy.24
  230.6 0.0 collective-permute-done.5
  230.6 1.4 fusion.2
  232.1 41.1 %all-to-all-done.3 = bf16[64,64,128]{2,1,0:T(8,128)(2,1)S(1)} async-done(((bf16[64,64,128]{2,1,0:T(8,128)(2,1)}), bf16[64,64,128]{2,1,0:T(8,128)(2,1)S(1)}, u32[]{:S(2)}, u32[]{:S(2)}) %all-to-all-start.3) | async-done | bytes 1048608 | tf_op jit(solution)/shard_map/all_to_all | solution.py:297
  273.1 2.4 fusion.6
  275.5 1.6 copy.18
  (12 shorter events, 0.1 us)
Async XLA Ops:
  0.6 31.0 %copy-start = (bf16[128,128]{1,0:T(8,128)(2,1)S(1)}, bf16[128,128]{1,0:T(8,128)(2,1)}, u32[]{:S(2)}) copy-start(bf16[128,128]{1,0:T(8,128)(2,1)} %param.9) | copy-start | bytes 98308
  0.6 2.0 copy-start.2
  0.7 2.0 copy-start.3
  0.7 2.0 copy-start.1
  4.7 20.3 %copy-start.6 = (bf16[64,64,128]{2,1,0:T(8,128)(2,1)S(1)}, bf16[64,64,128]{2,1,0:T(8,128)(2,1)}, u32[]{:S(2)}) copy-start(bf16[64,64,128]{2,1,0:T(8,128)(2,1)} %param.8) | copy-start | bytes 3145732
  5.9 25.4 %slice-start = ((bf16[64,64,128]{2,1,0:T(8,128)(2,1)}), bf16[64,56,128]{2,1,0:T(8,128)(2,1)S(1)}, s32[]{:S(2)}) async-start(bf16[64,64,128]{2,1,0:T(8,128)(2,1)} %param.8), calls=%async_computation.4 | async-start | bytes 1835008 | tf_op jit(solution)/shard_map/slice | solution.py:333
  5.9 85.5 %all-to-all-start = ((bf16[64,80,128]{2,1,0:T(8,128)(2,1)}), bf16[64,80,128]{2,1,0:T(8,128)(2,1)}, u32[]{:S(2)}, u32[]{:S(2)}) async-start(bf16[64,80,128]{2,1,0:T(8,128)(2,1)} %pad_maximum_fusion.1), calls=%async_computation | async-start | bytes 2621440 | tf_op jit(solution)/shard_map/all_to_all | solution.py:297
  25.0 6.3 %collective-permute-start = (bf16[64,8,128]{2,1,0:T(8,128)(2,1)S(1)}, bf16[64,8,128]{2,1,0:T(8,128)(2,1)S(1)}, u32[]{:S(2)}, u32[]{:S(2)}) collective-permute-start(bf16[64,8,128]{2,1,0:T(8,128)(2,1)S(1)} %slice.40), channel_id=1, source_target_pairs={{0,1},{1,2},{2,3},{3,4},{4,5},{5,6},{6,7},{8,9},{9,10},{10,11},{11... | collective-permute-start | bytes 393224 | tf_op jit(solution)/shard_map/ppermute | solution.py:23
  26.9 4.7 %copy-start.9 = (f32[128]{0:T(128)S(1)}, f32[128]{0:T(128)}, u32[]{:S(2)}) copy-start(f32[128]{0:T(128)} %param.10) | copy-start | bytes 1540
  33.3 2.1 copy-start.4
  37.2 76.2 %copy-start.8 = (bf16[64,192]{1,0:T(8,128)(2,1)S(1)}, bf16[64,192]{1,0:T(8,128)(2,1)}, u32[]{:S(2)}) copy-start(bf16[64,192]{1,0:T(8,128)(2,1)} %param.11) | copy-start | bytes 73732
  91.4 60.3 %all-to-all-start.1 = ((bf16[64,64,128]{2,1,0:T(8,128)(2,1)}), bf16[64,64,128]{2,1,0:T(8,128)(2,1)S(1)}, u32[]{:S(2)}, u32[]{:S(2)}) async-start(bf16[64,64,128]{2,1,0:T(8,128)(2,1)} %bitcast_bitcast_fusion), calls=%async_computation.1 | async-start | bytes 2097152 | tf_op jit(solution)/shard_map/all_to_all | solution.py:297
  98.1 9.8 %collective-permute-start.3 = (bf16[64,8,128]{2,1,0:T(8,128)(2,1)S(1)}, bf16[64,8,128]{2,1,0:T(8,128)(2,1)S(1)}, u32[]{:S(2)}, u32[]{:S(2)}) collective-permute-start(bf16[64,8,128]{2,1,0:T(8,128)(2,1)S(1)} %get-tuple-element.23), channel_id=1, source_target_pairs={{0,6},{1,7},{2,0},{3,1},{4,2},{5,3},{6,4},{7,5},{8,14},{9,15},{10,... | collective-permute-start | bytes 393224 | tf_op jit(solution)/shard_map/ppermute | solution.py:326
  100.9 8.4 %collective-permute-start.2 = (bf16[64,8,128]{2,1,0:T(8,128)(2,1)S(1)}, bf16[64,8,128]{2,1,0:T(8,128)(2,1)S(1)}, u32[]{:S(2)}, u32[]{:S(2)}) collective-permute-start(bf16[64,8,128]{2,1,0:T(8,128)(2,1)S(1)} %get-tuple-element.23), channel_id=1, source_target_pairs={{0,4},{1,5},{2,6},{3,7},{4,0},{5,1},{6,2},{7,3},{8,12},{9,13},{10,... | collective-permute-start | bytes 393224 | tf_op jit(solution)/shard_map/ppermute | solution.py:326
  103.9 7.2 %collective-permute-start.1 = (bf16[64,8,128]{2,1,0:T(8,128)(2,1)S(1)}, bf16[64,8,128]{2,1,0:T(8,128)(2,1)S(1)}, u32[]{:S(2)}, u32[]{:S(2)}) collective-permute-start(bf16[64,8,128]{2,1,0:T(8,128)(2,1)S(1)} %get-tuple-element.23), channel_id=1, source_target_pairs={{0,2},{1,3},{2,4},{3,5},{4,6},{5,7},{6,0},{7,1},{8,10},{9,11},{10,... | collective-permute-start | bytes 393224 | tf_op jit(solution)/shard_map/ppermute | solution.py:326
  111.2 3.8 %collective-permute-start.4 = (bf16[4,64,8,128]{3,2,1,0:T(8,128)(2,1)S(1)}, bf16[4,64,8,128]{3,2,1,0:T(8,128)(2,1)S(1)}, u32[]{:S(2)}, u32[]{:S(2)}) collective-permute-start(bf16[4,64,8,128]{3,2,1,0:T(8,128)(2,1)S(1)} %pad_maximum_fusion.2), channel_id=1, source_target_pairs={{0,1},{1,0},{2,3},{3,2},{4,5},{5,4},{6,7},{7,6},{8,9},{9,8},{10,11... | collective-permute-start | bytes 1572872 | tf_op jit(solution)/shard_map/ppermute | solution.py:329
  115.0 0.8 copy-start.10
  151.6 61.0 %all-to-all-start.2 = ((bf16[64,64,128]{2,1,0:T(8,128)(2,1)}), bf16[64,64,128]{2,1,0:T(8,128)(2,1)}, u32[]{:S(2)}, u32[]{:S(2)}) async-start(bf16[64,64,128]{2,1,0:T(8,128)(2,1)} %get-tuple-element.12), calls=%async_computation.2 | async-start | bytes 2097152 | tf_op jit(solution)/shard_map/all_to_all | solution.py:297
  175.6 43.1 %copy-start.7 = (bf16[64,64,128]{2,1,0:T(8,128)(2,1)S(1)}, bf16[64,64,128]{2,1,0:T(8,128)(2,1)}, u32[]{:S(2)}) copy-start(bf16[64,64,128]{2,1,0:T(8,128)(2,1)} %param.15) | copy-start | bytes 3145732
  212.6 60.5 %all-to-all-start.3 = ((bf16[64,64,128]{2,1,0:T(8,128)(2,1)}), bf16[64,64,128]{2,1,0:T(8,128)(2,1)S(1)}, u32[]{:S(2)}, u32[]{:S(2)}) async-start(bf16[64,64,128]{2,1,0:T(8,128)(2,1)} %forward_hops.1), calls=%async_computation.3 | async-start | bytes 2097152 | tf_op jit(solution)/shard_map/all_to_all | solution.py:297
  224.1 3.4 %copy-start.5 = (f32[128,8192]{1,0:T(8,128)S(1)}, f32[128,8192]{1,0:T(8,128)}, u32[]{:S(2)}) copy-start(f32[128,8192]{1,0:T(8,128)} %copy-done.4) | copy-start | bytes 12582916
  224.6 6.0 %collective-permute-start.5 = (bf16[64,8,128]{2,1,0:T(8,128)(2,1)S(1)}, bf16[64,8,128]{2,1,0:T(8,128)(2,1)S(1)}, u32[]{:S(2)}, u32[]{:S(2)}) collective-permute-start(bf16[64,8,128]{2,1,0:T(8,128)(2,1)S(1)} %slice.87), channel_id=1, source_target_pairs={{1,0},{2,1},{3,2},{4,3},{5,4},{6,5},{7,6},{9,8},{10,9},{11,10},{12... | collective-permute-start | bytes 393224 | tf_op jit(solution)/shard_map/ppermute | solution.py:23
